TPU v7x, 32 devices: a whole 2x2x4 slice. The times are simulated.
32 devices in a mesh: dp: 2 (over y), shard: 16 (over z, x, core).
Axes of the slice: x: 2, y: 2, z: 4, core: 2. Of those that a mesh axis runs over, the one named last changes fastest.
Arguments:
- queries: bfloat16 [8192, 1024], P(('dp', 'shard')), may hold values from -16 to 16
- passages: bfloat16 [8192, 1024], P(('dp', 'shard')), may hold values from -5 to 5
- block_lists: int32 [32, 4], P('dp'), may hold values from 0 to 15, as said below
- inv_temp: float32 [], replicated, may hold values from 0.02 to 0.05
Outputs:
- query_grad: bfloat16 [8192, 1024], P(('dp', 'shard'))
- passage_grad: bfloat16 [8192, 1024], P(('dp', 'shard'))
- loss_mean: float32 [], replicated
- temp_grad: float32 [], replicated
Inputs may be any that keep to these rules, and one draw needn't show every extreme that they name: `block_lists`: column 0 of row t * 16 + s names the positive passage block and columns 1 to 3 the negative passage blocks of query block t * 16 + s, as numbers within data group t; a row's numbers are distinct; the positives of one group's query blocks are a permutation of its 16 blocks.
All inputs are finite; a program needn't handle non-finite values.
Results may differ from a plain program's by a relative error of at most 0.0041.
Values may be sent and summed in bfloat16 or wider, within the bound.
A program may use at most 64 MiB of HBM per device.

v0:
```python
import jax
import jax.numpy as jnp
from jax import lax
from jax.sharding import PartitionSpec as P


def local(queries, passages, block_lists, inv_temp):
    shard_count = lax.axis_size("shard")
    row_count, feat_width = passages.shape
    listed = block_lists.shape[1]
    col_piece = feat_width // shard_count
    outgoing = passages.reshape(row_count, shard_count, col_piece).transpose(1, 0, 2)
    stripes = lax.all_to_all(outgoing, "shard", split_axis=0, concat_axis=0, tiled=True)
    requests = stripes[block_lists]
    fetched = lax.all_to_all(requests, "shard", split_axis=0, concat_axis=3, tiled=True)
    logits = inv_temp * jnp.einsum(
        "qd,mkd->mqk", queries, fetched[0], preferred_element_type=jnp.float32
    )
    fetched, logits = (fetched, logits[None])
    key_rows = fetched[0]
    logits = logits[0]
    row_peak = jnp.max(logits, axis=(0, 2))
    exp_terms = jnp.exp(logits - row_peak[None, :, None])
    exp_total = jnp.sum(exp_terms, axis=(0, 2))
    row_loss = row_peak + jnp.log(exp_total) - jnp.diagonal(logits[0])
    first_block = (jnp.arange(listed, dtype=jnp.int32) == 0).astype(jnp.float32)
    target = first_block[:, None, None] * jnp.eye(row_count, dtype=jnp.float32)[None]
    residual = exp_terms / exp_total[None, :, None] - target
    weights = residual.astype(jnp.bfloat16)
    temp_part = jnp.sum(residual * logits) / inv_temp
    block_grad = (
        inv_temp * jnp.einsum("mqk,qd->mkd", weights, queries, preferred_element_type=jnp.float32)
    ).astype(jnp.bfloat16)[None]
    query_grad = (
        inv_temp * jnp.einsum("mqk,mkd->qd", weights, key_rows, preferred_element_type=jnp.float32)
    ).astype(jnp.bfloat16)
    block_index = jnp.arange(shard_count, dtype=jnp.int32)
    onehot = (block_lists.reshape(-1)[None, :] == block_index[:, None]).astype(jnp.bfloat16)
    returned = lax.all_to_all(block_grad, "shard", split_axis=3, concat_axis=0, tiled=True)
    summed = jnp.dot(
        onehot,
        returned.reshape(shard_count * listed, row_count * col_piece),
        preferred_element_type=jnp.float32,
    )
    settled = summed.astype(jnp.bfloat16).reshape(shard_count, row_count, col_piece)
    arrived = lax.all_to_all(settled, "shard", split_axis=0, concat_axis=0, tiled=True)
    passage_grad = arrived.transpose(1, 0, 2).reshape(row_count, feat_width)
    totals = lax.psum((jnp.sum(row_loss), temp_part), ("dp", "shard"))
    pair_count = row_count * lax.axis_size("dp") * shard_count
    loss_mean = totals[0] / pair_count
    temp_grad = totals[1] / pair_count
    return (query_grad, passage_grad, loss_mean, temp_grad)


def solution(mesh):
    placed = (P(("dp", "shard"), None), P(("dp", "shard"), None), P("dp", None), P())
    return jax.shard_map(
        local,
        mesh=mesh,
        in_specs=placed,
        out_specs=(P(("dp", "shard"), None), P(("dp", "shard"), None), P(), P()),
        check_vma=False,
    )
```

profile of v0, /device:TPU:0, one launch (start us, length us, event | category | flops | bytes accessed | tf_op | source)
XLA Modules:
  0.0 208.5 jit_solution(15300739401027454315)
XLA Ops:
  0.6 0.0 copy-start
  0.6 0.0 copy-start.6
  0.7 2.1 %copy.23 = bf16[256,1024]{0,1:T(8,128)(2,1)} copy(bf16[256,1024]{1,0:T(8,128)(2,1)} %param.5) | data formatting | bytes 1048576 | tf_op args[1]
  2.8 7.4 %all-to-all-start = ((bf16[16,256,64]{1,2,0:T(8,128)(2,1)}), bf16[16,256,64]{1,2,0:T(8,128)(2,1)S(1)}, u32[]{:S(2)}, u32[]{:S(2)}) async-start(bf16[16,256,64]{1,2,0:T(8,128)(2,1)} %bitcast.1), calls=%async_computation | async-start | bytes 1048576 | tf_op jit(solution)/shard_map/all_to_all | solution.py:13
  10.1 0.0 copy-done.6
  10.1 0.1 copy.24
  10.2 0.1 reshape.44
  10.3 14.3 %all-to-all-done = bf16[16,256,64]{1,2,0:T(8,128)(2,1)S(1)} async-done(((bf16[16,256,64]{1,2,0:T(8,128)(2,1)}), bf16[16,256,64]{1,2,0:T(8,128)(2,1)S(1)}, u32[]{:S(2)}, u32[]{:S(2)}) %all-to-all-start) | async-done | bytes 524320 | tf_op jit(solution)/shard_map/all_to_all | solution.py:13
  24.6 2.0 gather_fusion
  26.6 4.1 %all-to-all-start.1 = ((bf16[16,4,256,64]{2,3,1,0:T(8,128)(2,1)}), bf16[16,4,256,64]{2,3,1,0:T(8,128)(2,1)S(1)}, u32[]{:S(2)}, u32[]{:S(2)}) async-start(bf16[16,4,256,64]{2,3,1,0:T(8,128)(2,1)} %bitcast.2), calls=%async_computation.1 | async-start | bytes 4194304 | tf_op jit(solution)/shard_map/all_to_all | solution.py:15
  31.4 0.0 copy-start.4
  31.4 40.4 %all-to-all-done.1 = bf16[16,4,256,64]{2,3,1,0:T(8,128)(2,1)S(1)} async-done(((bf16[16,4,256,64]{2,3,1,0:T(8,128)(2,1)}), bf16[16,4,256,64]{2,3,1,0:T(8,128)(2,1)S(1)}, u32[]{:S(2)}, u32[]{:S(2)}) %all-to-all-start.1) | async-done | bytes 2097184 | tf_op jit(solution)/shard_map/all_to_all | solution.py:15
  71.8 0.1 copy.25
  72.0 0.0 copy-start.3
  72.0 1.3 copy-done.3
  73.3 0.0 copy-done
  73.3 0.8 fusion.11
  74.1 0.0 copy-start.1
  74.1 0.2 fusion.3
  74.3 0.0 copy-done.4
  74.3 0.8 copy-done.1
  75.1 0.8 fusion
  75.8 2.6 %copy.30 = bf16[1,4,256,1024]{2,1,0,3:T(4,128)(2,1)} copy(bf16[1,4,256,1024]{3,2,1,0:T(8,128)(2,1)S(1)} %fusion) | data formatting | bytes 4194304 | tf_op jit(solution)/shard_map/broadcast_in_dim | solution.py:31
  78.5 11.3 %all-to-all-start.2 = ((bf16[1,4,256,1024]{2,1,0,3:T(4,128)(2,1)}), bf16[1,4,256,1024]{2,1,0,3:T(4,128)(2,1)}, u32[]{:S(2)}, u32[]{:S(2)}) async-start(bf16[1,4,256,1024]{2,1,0,3:T(4,128)(2,1)} %copy.30), calls=%async_computation.2 | async-start | bytes 4194304 | tf_op jit(solution)/shard_map/all_to_all | solution.py:39
  89.7 0.1 copy.29
  89.8 0.1 eq.31
  89.9 41.0 %all-to-all-done.2 = bf16[1,4,256,1024]{2,1,0,3:T(4,128)(2,1)} async-done(((bf16[1,4,256,1024]{2,1,0,3:T(4,128)(2,1)}), bf16[1,4,256,1024]{2,1,0,3:T(4,128)(2,1)}, u32[]{:S(2)}, u32[]{:S(2)}) %all-to-all-start.2) | async-done | bytes 2097184 | tf_op jit(solution)/shard_map/all_to_all | solution.py:39
  130.9 1.9 copy.31
  132.8 3.2 %copy.32 = bf16[16,1,4,256,64]{4,3,2,0,1:T(8,128)(2,1)} copy(bf16[16,1,4,256,64]{3,4,0,2,1:T(8,128)(2,1)S(1)} %bitcast.46) | data formatting | bytes 4194304 | tf_op jit(solution)/shard_map/all_to_all | solution.py:39
  135.9 5.0 %reshape.39 = bf16[64,16384]{1,0:T(8,128)(2,1)S(1)} reshape(bf16[16,1,4,256,64]{4,3,2,0,1:T(8,128)(2,1)} %copy.32) | data formatting | bytes 4194304 | tf_op jit(solution)/shard_map/reshape | solution.py:42
  140.9 0.4 convolution_convert_fusion
  141.3 0.0 copy-start.2
  141.3 1.1 reshape.40
  142.4 0.0 copy-start.5
  142.4 1.1 copy.33
  143.6 11.2 %all-to-all-start.3 = ((bf16[16,256,64]{1,2,0:T(8,128)(2,1)}), bf16[16,256,64]{1,2,0:T(8,128)(2,1)S(1)}, u32[]{:S(2)}, u32[]{:S(2)}) async-start(bf16[16,256,64]{1,2,0:T(8,128)(2,1)} %copy.33), calls=%async_computation.3 | async-start | bytes 1048576 | tf_op jit(solution)/shard_map/all_to_all | solution.py:46
  154.8 0.0 copy-done.2
  154.8 2.4 %gather_fusion.1 = f32[256]{0:T(256)S(1)} fusion(f32[256,256]{0,1:T(8,128)S(1)} %slice_bitcast_fusion, s32[256]{0:T(256)S(1)} %bitcast.45), kind=kCustom, calls=%fused_computation.1 | custom fusion | bytes 4096 | tf_op jit(solution)/shard_map/jit(diagonal)/cond/branch_0_fun/gather | solution.py:25
  157.2 0.6 subtract_reduce_fusion
  157.8 0.0 copy-done.5
  157.8 1.0 multiply_reduce_fusion
  159.5 41.1 %all-reduce = (f32[]{:T(128)}, f32[]{:T(128)}) all-reduce(f32[]{:T(128)} %subtract_reduce_fusion, f32[]{:T(128)S(6)} %div.20), channel_id=1, replica_groups=mesh['dp'=2,'shard'=16] {'dp','shard'}, use_global_device_ids=true, to_apply=%region_3.4 | all-reduce | flops 2 | bytes 16 | tf_op jit(solution)/shard_map/psum | solution.py:48
  201.9 3.3 %fusion.2 = bf16[256,1024]{1,0:T(8,128)(2,1)} fusion(bf16[4,256,1024]{1,2,0:T(8,128)(2,1)} %bitcast.50, f32[]{:T(128)S(6)} %copy.38, f32[256,256]{0,1:T(8,128)S(1)} %copy-done.5, f32[4]{0:T(128)S(1)} %compare_convert_fusion, f32[256]{0:T(256)S(1)} %fusion.3, f32[256]{0:T(256)S(1)} %get-tuple-element.14, f32[4,256,256]{2,1,0:T(8,128)S(1)} %copy-done.2), kind=kOutput, calls=%fused_computation.8 | convolution fusion | flops 538705920 | bytes 3934228 | tf_op jit(solution)/shard_map/mqk,mkd->qd/dot_general | solution.py:35
  205.2 0.0 all-to-all-done.3
  205.2 1.0 copy.34
  (6 shorter events, 0.1 us)
Async XLA Ops:
  0.6 72.6 %copy-start = (bf16[256,1024]{1,0:T(8,128)(2,1)S(1)}, bf16[256,1024]{1,0:T(8,128)(2,1)}, u32[]{:S(2)}) copy-start(bf16[256,1024]{1,0:T(8,128)(2,1)} %param.4) | copy-start | bytes 1572868
  0.6 9.5 %copy-start.6 = (s32[16,4]{0,1:T(4,128)S(1)}, s32[16,4]{0,1:T(4,128)}, u32[]{:S(2)}) copy-start(s32[16,4]{0,1:T(4,128)} %param.6) | copy-start | bytes 772
  2.8 21.8 %all-to-all-start = ((bf16[16,256,64]{1,2,0:T(8,128)(2,1)}), bf16[16,256,64]{1,2,0:T(8,128)(2,1)S(1)}, u32[]{:S(2)}, u32[]{:S(2)}) async-start(bf16[16,256,64]{1,2,0:T(8,128)(2,1)} %bitcast.1), calls=%async_computation | async-start | bytes 1048576 | tf_op jit(solution)/shard_map/all_to_all | solution.py:13
  26.6 45.2 %all-to-all-start.1 = ((bf16[16,4,256,64]{2,3,1,0:T(8,128)(2,1)}), bf16[16,4,256,64]{2,3,1,0:T(8,128)(2,1)S(1)}, u32[]{:S(2)}, u32[]{:S(2)}) async-start(bf16[16,4,256,64]{2,3,1,0:T(8,128)(2,1)} %bitcast.2), calls=%async_computation.1 | async-start | bytes 4194304 | tf_op jit(solution)/shard_map/all_to_all | solution.py:15
  31.4 42.9 %copy-start.4 = (f32[256,256]{0,1:T(8,128)}, f32[256,256]{0,1:T(8,128)S(1)}, u32[]{:S(2)}) copy-start(f32[256,256]{0,1:T(8,128)S(1)} %fusion.7) | copy-start | bytes 786436
  72.0 1.3 copy-start.3
  74.1 1.0 copy-start.1
  78.5 52.4 %all-to-all-start.2 = ((bf16[1,4,256,1024]{2,1,0,3:T(4,128)(2,1)}), bf16[1,4,256,1024]{2,1,0,3:T(4,128)(2,1)}, u32[]{:S(2)}, u32[]{:S(2)}) async-start(bf16[1,4,256,1024]{2,1,0,3:T(4,128)(2,1)} %copy.30), calls=%async_computation.2 | async-start | bytes 4194304 | tf_op jit(solution)/shard_map/all_to_all | solution.py:39
  141.3 13.5 %copy-start.2 = (f32[4,256,256]{2,1,0:T(8,128)S(1)}, f32[4,256,256]{2,1,0:T(8,128)}, u32[]{:S(2)}) copy-start(f32[4,256,256]{2,1,0:T(8,128)} %copy-done.1) | copy-start | bytes 3145732
  142.4 15.4 %copy-start.5 = (f32[256,256]{0,1:T(8,128)S(1)}, f32[256,256]{0,1:T(8,128)}, u32[]{:S(2)}) copy-start(f32[256,256]{0,1:T(8,128)} %copy-done.4) | copy-start | bytes 786436
  143.6 61.6 %all-to-all-start.3 = ((bf16[16,256,64]{1,2,0:T(8,128)(2,1)}), bf16[16,256,64]{1,2,0:T(8,128)(2,1)S(1)}, u32[]{:S(2)}, u32[]{:S(2)}) async-start(bf16[16,256,64]{1,2,0:T(8,128)(2,1)} %copy.33), calls=%async_computation.3 | async-start | bytes 1048576 | tf_op jit(solution)/shard_map/all_to_all | solution.py:46
where the time goes:
time: 209 us; the launch traced here: 208 us
  waiting for transfers between devices  95.6 us (46%)
  blocking collectives  41.1 us (20%)
  starting transfers between devices  33.9 us (16%)
  local copies, waits for them, and re-layouts  25 us (12%)
  between operations  5.71 us (3%)
  matrix products  5.25 us (3%)
    psum x1, blocking collectives, local(): totals = lax.psum((jnp.sum(row_loss), temp_part), ('dp', 'shard'))  41.1 us
    all_to_all x1, waiting for transfers between devices, local(): lax.all_to_all(block_grad, 'shard', split_axis=3, concat_axis=0, tiled=True)  41 us
    all_to_all x1, waiting for transfers between devices, local(): lax.all_to_all(requests, 'shard', split_axis=0, concat_axis=3, tiled=True)  40.4 us
    all_to_all x1, waiting for transfers between devices, local(): lax.all_to_all(outgoing, 'shard', split_axis=0, concat_axis=0, tiled=True)  14.3 us
    all_to_all x1, starting transfers between devices, local(): lax.all_to_all(block_grad, 'shard', split_axis=3, concat_axis=0, tiled=True)  11.3 us
    all_to_all x1, starting transfers between devices, local(): lax.all_to_all(settled, 'shard', split_axis=0, concat_axis=0, tiled=True)  11.2 us
    all_to_all x1, starting transfers between devices, local(): lax.all_to_all(outgoing, 'shard', split_axis=0, concat_axis=0, tiled=True)  7.36 us
    unnamed x17, local copies, waits for them, and re-layouts  5.3 us
  transfers between devices with their start and end apart: 4, of which 3 were waited for; matrix products, arithmetic and copies ran while one was open for 4% of the time, Pallas kernels for 0%

commit v1 on v0

--- a/solution.py
+++ b/solution.py
@@ -1,10 +1,424 @@
+import functools
+
 import jax
 import jax.numpy as jnp
 from jax import lax
+from jax.experimental import pallas as pl
+from jax.experimental.pallas import tpu as pltpu
 from jax.sharding import PartitionSpec as P
 
-
-def local(queries, passages, block_lists, inv_temp):
+MESH = pl.DeviceIdType.MESH
+LOW = -1e30
+NT = (((1,), (1,)), ((), ()))
+TN = (((0,), (0,)), ((), ()))
+NN = (((1,), (0,)), ((), ()))
+
+
+def dot(a, b, dims):
+    return lax.dot_general(a, b, dims, preferred_element_type=jnp.float32)
+
+
+def kernel(line, groups, q_in, p_in, lists, temp, qg_out, pg_out, tot_out,
+           pcol, qcat, ebuf, wbuf, mrec, stat, stat_in, chip_in, own, zin_r, zin_l,
+           zsend, psend, qsend, qrecv, acc, acc_in,
+           loc_sem, q_sems, p_recv, p_right, p_left, p_core, st_sems,
+           c_send, c_recv, r_send, r_recv, l_send, l_recv, g_sems, a_send, a_recv):
+    rows = q_in.shape[0]
+    listed = lists.shape[1]
+    dp = lax.axis_index("dp")
+    me = lax.axis_index("shard")
+    k = lax.rem(me, 2)
+    x = lax.rem(me // 2, 2)
+    z = me // 4
+
+    def dev(zz, xx, kk):
+        return (dp, (zz * 2 + xx) * 2 + kk)
+
+    core = dev(z, x, 1 - k)
+    mate = dev(z, 1 - x, k)
+    right = dev(lax.rem(z + 1, line), x, k)
+    left = dev(lax.rem(z + line - 1, line), x, k)
+    has_r = z < line - 1
+    has_l = z > 0
+    pairs = [core, mate]
+    bit = 1
+    far = []
+    while bit < line:
+        other = z + bit - 2 * bit * lax.rem(z // bit, 2)
+        pairs.append(dev(other, x, k))
+        if bit > 1:
+            far.append(dev(other, x, k))
+        bit *= 2
+    bit = 1
+    while bit < groups:
+        other = dp + bit - 2 * bit * lax.rem(dp // bit, 2)
+        pairs.append((other, me))
+        far.append((other, me))
+        bit *= 2
+
+    mine = z * 2 + k
+    own_p = pltpu.make_async_copy(p_in, pcol.at[mine], loc_sem.at[0])
+    own_q = pltpu.make_async_copy(q_in, qcat.at[pl.ds(x * rows, rows)], loc_sem.at[1])
+    own_p.start()
+    own_q.start()
+
+    barrier = pltpu.get_barrier_semaphore()
+    for d in [core, mate] + far:
+        pl.semaphore_signal(barrier, inc=1, device_id=d, device_id_type=MESH)
+
+    @pl.when(has_r)
+    def _():
+        pl.semaphore_signal(barrier, inc=1, device_id=right, device_id_type=MESH)
+
+    @pl.when(has_l)
+    def _():
+        pl.semaphore_signal(barrier, inc=1, device_id=left, device_id_type=MESH)
+
+    ends = jnp.where(has_r, 1, 0) + jnp.where(has_l, 1, 0)
+    pl.semaphore_wait(barrier, 2 + len(far) + ends)
+
+    def remote(src, dst, send, recv, d):
+        return pltpu.make_async_remote_copy(
+            src_ref=src, dst_ref=dst, send_sem=send, recv_sem=recv,
+            device_id=d, device_id_type=MESH)
+
+    def p_copy(zz, sems, d):
+        slot = zz * 2 + k
+        return remote(pcol.at[slot], pcol.at[slot], sems.at[zz], p_recv.at[slot], d)
+
+    def p_wait(slot):
+        remote(pcol.at[slot], pcol.at[slot], p_core.at[0], p_recv.at[slot], core).wait_recv()
+
+    my_rows = pl.ds(x * rows, rows)
+    q_copy = remote(qcat.at[my_rows], qcat.at[my_rows], q_sems.at[0], q_sems.at[1], mate)
+    mate_rows = pl.ds((1 - x) * rows, rows)
+    q_wait = remote(qcat.at[mate_rows], qcat.at[mate_rows], q_sems.at[0], q_sems.at[1], mate)
+
+    own_p.wait()
+
+    @pl.when(has_r)
+    def _():
+        p_copy(z, p_right, right).start()
+
+    @pl.when(has_l)
+    def _():
+        p_copy(z, p_left, left).start()
+
+    own_q.wait()
+    q_copy.start()
+    p_copy(z, p_core, core).start()
+
+    lane = lax.broadcasted_iota(jnp.int32, (1, 2 * rows), 1)
+    jj = lax.broadcasted_iota(jnp.int32, (rows, 2 * rows), 0)
+    ii = lax.broadcasted_iota(jnp.int32, (rows, 2 * rows), 1)
+    eye = jj == jnp.where(ii < rows, ii, ii - rows)
+    inv_temp = temp[0]
+    row_a = z * 4 + k
+    row_b = z * 4 + 2 + k
+
+    def per_lane(block_id, first, last):
+        a = jnp.int32(0)
+        b = jnp.int32(0)
+        for m in range(first, last):
+            a = a + jnp.where(lists[row_a, m] == block_id, 1, 0)
+            b = b + jnp.where(lists[row_b, m] == block_id, 1, 0)
+        return jnp.where(lane < rows, a, b)
+
+    def block_of(slot):
+        return (slot // 2) * 4 + x * 2 + lax.rem(slot, 2)
+
+    stat[0:1, :] = jnp.full((1, 2 * rows), LOW, jnp.float32)
+    stat[1:8, :] = jnp.zeros((7, 2 * rows), jnp.float32)
+
+    def consume(slot):
+        ident = block_of(slot)
+        live = per_lane(ident, 0, listed) > 0
+        pos = per_lane(ident, 0, 1) > 0
+        s = dot(pcol[slot], qcat[...], NT) * inv_temp
+        s = jnp.where(live, s, LOW)
+        m_old = stat[0:1, :]
+        m_new = jnp.maximum(m_old, jnp.max(s, axis=0, keepdims=True))
+        e = jnp.exp(s - m_new)
+        ebuf[slot] = e
+        scale = jnp.exp(m_old - m_new)
+        stat[0:1, :] = m_new
+        stat[1:2, :] = stat[1:2, :] * scale + jnp.sum(e, axis=0, keepdims=True)
+        stat[2:3, :] = stat[2:3, :] * scale + jnp.sum(e * s, axis=0, keepdims=True)
+        diag = jnp.sum(jnp.where(eye, s, 0.0), axis=0, keepdims=True)
+        stat[3:4, :] = stat[3:4, :] + jnp.where(pos, diag, 0.0)
+        mrec[slot] = jnp.broadcast_to(m_new, (8, 2 * rows))
+
+    q_wait.wait_recv()
+
+    @pl.loop(0, line - 1)
+    def _(s):
+        from_l = z - 1 - s
+        from_r = z + 1 + s
+
+        @pl.when(from_l >= 0)
+        def _():
+            p_wait(from_l * 2 + k)
+
+            @pl.when(has_r)
+            def _():
+                p_copy(from_l, p_right, right).start()
+
+            p_copy(from_l, p_core, core).start()
+
+        @pl.when(from_r < line)
+        def _():
+            p_wait(from_r * 2 + k)
+
+            @pl.when(has_l)
+            def _():
+                p_copy(from_r, p_left, left).start()
+
+            p_copy(from_r, p_core, core).start()
+
+        @pl.when(s == 0)
+        def _():
+            consume(mine)
+            p_wait(z * 2 + 1 - k)
+            consume(z * 2 + 1 - k)
+
+        @pl.when(from_l >= 0)
+        def _():
+            consume(from_l * 2 + k)
+            p_wait(from_l * 2 + 1 - k)
+            consume(from_l * 2 + 1 - k)
+
+        @pl.when(from_r < line)
+        def _():
+            consume(from_r * 2 + k)
+            p_wait(from_r * 2 + 1 - k)
+            consume(from_r * 2 + 1 - k)
+
+    st_copy = remote(stat, stat_in, st_sems.at[0], st_sems.at[1], mate)
+    st_copy.start()
+    st_copy.wait_recv()
+    m_loc = stat[0:1, :]
+    m_in = stat_in[0:1, :]
+    peak = jnp.maximum(m_loc, m_in)
+    total = stat[1:2, :] * jnp.exp(m_loc - peak) + stat_in[1:2, :] * jnp.exp(m_in - peak)
+    inv_total = 1.0 / total
+
+    def make_w(slot):
+        pos = per_lane(block_of(slot), 0, 1) > 0
+        scale = jnp.exp(mrec[slot][0:1, :] - peak) * inv_total
+        target = jnp.where(jnp.logical_and(eye, pos), 1.0, 0.0)
+        w = (ebuf[slot] * scale - target).astype(jnp.bfloat16)
+        wbuf[slot] = w
+        return w
+
+    def p_grad(slot):
+        return dot(make_w(slot), qcat[...], NN) * inv_temp
+
+    def c_copy(d):
+        return remote(psend.at[d], chip_in.at[d], c_send.at[d], c_recv.at[d], core)
+
+    def r_copy(d):
+        return remote(zsend.at[d], zin_r.at[d], r_send.at[d], r_recv.at[d], right)
+
+    def l_copy(d):
+        return remote(zsend.at[d], zin_l.at[d], l_send.at[d], l_recv.at[d], left)
+
+    def give(d):
+        psend[d] = p_grad(d * 2 + 1 - k).astype(jnp.bfloat16)
+        c_copy(d).start()
+
+    def take(d):
+        own[d] = p_grad(d * 2 + k)
+        c_copy(d).wait_recv()
+        own[d] = own[d] + chip_in[d].astype(jnp.float32)
+
+    @pl.loop(0, line - 1)
+    def _(s):
+        dr = line - 1 - s
+        dl = s
+
+        @pl.when(dr > z)
+        def _():
+            give(dr)
+
+        @pl.when(dl < z)
+        def _():
+            give(dl)
+
+        @pl.when(dr > z)
+        def _():
+            take(dr)
+
+            @pl.when(z == 0)
+            def _():
+                zsend[dr] = own[dr].astype(jnp.bfloat16)
+                r_copy(dr).start()
+
+        @pl.when(dl < z)
+        def _():
+            take(dl)
+
+            @pl.when(z == line - 1)
+            def _():
+                zsend[dl] = own[dl].astype(jnp.bfloat16)
+                l_copy(dl).start()
+
+    give(z)
+    take(z)
+
+    def q_part(start):
+        part = jnp.zeros((rows, q_in.shape[1]), jnp.float32)
+        for c in range(2 * line):
+            part = part + dot(wbuf[c, :, pl.ds(start, rows)], pcol[c], TN)
+        return part * inv_temp
+
+    @pl.when(x == 0)
+    def _():
+        qsend[...] = q_part(rows).astype(jnp.bfloat16)
+
+    @pl.when(x == 1)
+    def _():
+        qsend[...] = q_part(0).astype(jnp.bfloat16)
+
+    g_copy = remote(qsend, qrecv, g_sems.at[0], g_sems.at[1], mate)
+    g_copy.start()
+
+    owner = (lane >= x * rows) & (lane < x * rows + rows)
+    diag = stat[3:4, :]
+    loss = jnp.where(owner, peak + jnp.log(total), 0.0) - diag
+    grad = stat[2:3, :] * (jnp.exp(m_loc - peak) * inv_total) - diag
+    loss = jnp.sum(loss, axis=1, keepdims=True)
+    grad = jnp.sum(grad, axis=1, keepdims=True) / inv_temp
+    tile_row = lax.broadcasted_iota(jnp.int32, (8, 128), 0)
+    acc[0] = jnp.where(tile_row == 0, loss, grad)
+    a_copies = []
+    for i, d in enumerate(pairs):
+        copy = remote(acc.at[i], acc_in.at[i], a_send.at[i], a_recv.at[i], d)
+        copy.start()
+        copy.wait_recv()
+        acc[i + 1] = acc[i] + acc_in[i]
+        a_copies.append(copy)
+    tot_out[...] = acc[len(pairs)]
+
+    @pl.when(x == 0)
+    def _():
+        qg_out[...] = q_part(0).astype(jnp.bfloat16)
+
+    @pl.when(x == 1)
+    def _():
+        qg_out[...] = q_part(rows).astype(jnp.bfloat16)
+
+    @pl.loop(0, line - 1)
+    def _(s):
+        dr = line - 1 - s
+        dl = s
+
+        @pl.when((dr > z) & has_l)
+        def _():
+            r_copy(dr).wait_recv()
+            zsend[dr] = (own[dr] + zin_r[dr].astype(jnp.float32)).astype(jnp.bfloat16)
+            r_copy(dr).start()
+
+        @pl.when((dl < z) & has_r)
+        def _():
+            l_copy(dl).wait_recv()
+            zsend[dl] = (own[dl] + zin_l[dl].astype(jnp.float32)).astype(jnp.bfloat16)
+            l_copy(dl).start()
+
+    g_copy.wait_recv()
+    qg_out[...] = (qg_out[...].astype(jnp.float32) + qrecv[...].astype(jnp.float32)).astype(jnp.bfloat16)
+
+    @pl.when(has_l)
+    def _():
+        r_copy(z).wait_recv()
+        own[z] = own[z] + zin_r[z].astype(jnp.float32)
+
+    @pl.when(has_r)
+    def _():
+        l_copy(z).wait_recv()
+        own[z] = own[z] + zin_l[z].astype(jnp.float32)
+
+    pg_out[...] = own[z].astype(jnp.bfloat16)
+
+    q_copy.wait_send()
+    st_copy.wait_send()
+    g_copy.wait_send()
+    for copy in a_copies:
+        copy.wait_send()
+
+    @pl.loop(0, line)
+    def _(d):
+        p_copy(d, p_core, core).wait_send()
+        c_copy(d).wait_send()
+
+        @pl.when((d <= z) & has_r)
+        def _():
+            p_copy(d, p_right, right).wait_send()
+
+        @pl.when((d >= z) & has_l)
+        def _():
+            p_copy(d, p_left, left).wait_send()
+
+        @pl.when(d > z)
+        def _():
+            r_copy(d).wait_send()
+
+        @pl.when(d < z)
+        def _():
+            l_copy(d).wait_send()
+
+
+def fused(line, groups, queries, passages, block_lists, inv_temp):
+    rows, width = passages.shape
+    stages = 2 + (line.bit_length() - 1) + (groups.bit_length() - 1)
+    bf, f32 = jnp.bfloat16, jnp.float32
+    block = (rows, width)
+    vm, dma = pltpu.VMEM, pltpu.SemaphoreType.DMA
+    scratch = [
+        vm((2 * line,) + block, bf),
+        vm((2 * rows, width), bf),
+        vm((2 * line, rows, 2 * rows), f32),
+        vm((2 * line, rows, 2 * rows), bf),
+        vm((2 * line, 8, 2 * rows), f32),
+        vm((8, 2 * rows), f32),
+        vm((8, 2 * rows), f32),
+        vm((line,) + block, bf),
+        vm((line,) + block, f32),
+        vm((line,) + block, bf),
+        vm((line,) + block, bf),
+        vm((line,) + block, bf),
+        vm((line,) + block, bf),
+        vm(block, bf),
+        vm(block, bf),
+        vm((stages + 1, 8, 128), f32),
+        vm((stages, 8, 128), f32),
+        dma((2,)), dma((2,)), dma((2 * line,)), dma((line,)), dma((line,)), dma((line,)), dma((2,)),
+        dma((line,)), dma((line,)), dma((line,)), dma((line,)), dma((line,)), dma((line,)),
+        dma((2,)), dma((stages,)), dma((stages,)),
+    ]
+    query_grad, passage_grad, totals = pl.pallas_call(
+        functools.partial(kernel, line, groups),
+        out_shape=(
+            jax.ShapeDtypeStruct(block, bf),
+            jax.ShapeDtypeStruct(block, bf),
+            jax.ShapeDtypeStruct((8, 128), f32),
+        ),
+        in_specs=[
+            pl.BlockSpec(memory_space=pl.ANY),
+            pl.BlockSpec(memory_space=pl.ANY),
+            pl.BlockSpec(memory_space=pltpu.SMEM),
+            pl.BlockSpec(memory_space=pltpu.SMEM),
+        ],
+        out_specs=(pl.BlockSpec(memory_space=pltpu.VMEM),) * 3,
+        scratch_shapes=scratch,
+        compiler_params=pltpu.CompilerParams(
+            collective_id=0, has_side_effects=True, vmem_limit_bytes=56 * 1024 * 1024
+        ),
+    )(queries, passages, block_lists, inv_temp.reshape(1))
+    pair_count = rows * groups * line * 4
+    return query_grad, passage_grad, totals[0, 0] / pair_count, totals[1, 0] / pair_count
+
+
+def plain(queries, passages, block_lists, inv_temp):
     shard_count = lax.axis_size("shard")
     row_count, feat_width = passages.shape
     listed = block_lists.shape[1]
@@ -13,12 +427,10 @@
     stripes = lax.all_to_all(outgoing, "shard", split_axis=0, concat_axis=0, tiled=True)
     requests = stripes[block_lists]
     fetched = lax.all_to_all(requests, "shard", split_axis=0, concat_axis=3, tiled=True)
+    key_rows = fetched[0]
     logits = inv_temp * jnp.einsum(
-        "qd,mkd->mqk", queries, fetched[0], preferred_element_type=jnp.float32
+        "qd,mkd->mqk", queries, key_rows, preferred_element_type=jnp.float32
     )
-    fetched, logits = (fetched, logits[None])
-    key_rows = fetched[0]
-    logits = logits[0]
     row_peak = jnp.max(logits, axis=(0, 2))
     exp_terms = jnp.exp(logits - row_peak[None, :, None])
     exp_total = jnp.sum(exp_terms, axis=(0, 2))
@@ -47,15 +459,17 @@
     passage_grad = arrived.transpose(1, 0, 2).reshape(row_count, feat_width)
     totals = lax.psum((jnp.sum(row_loss), temp_part), ("dp", "shard"))
     pair_count = row_count * lax.axis_size("dp") * shard_count
-    loss_mean = totals[0] / pair_count
-    temp_grad = totals[1] / pair_count
-    return (query_grad, passage_grad, loss_mean, temp_grad)
+    return query_grad, passage_grad, totals[0] / pair_count, totals[1] / pair_count
 
 
 def solution(mesh):
+    shard_count, groups = mesh.shape["shard"], mesh.shape["dp"]
+    line = shard_count // 4
+    short = shard_count % 4 == 0 and 2 <= line <= 4 and line & (line - 1) == 0
+    body = functools.partial(fused, line, groups) if short and groups & (groups - 1) == 0 else plain
     placed = (P(("dp", "shard"), None), P(("dp", "shard"), None), P("dp", None), P())
     return jax.shard_map(
-        local,
+        body,
         mesh=mesh,
         in_specs=placed,
         out_specs=(P(("dp", "shard"), None), P(("dp", "shard"), None), P(), P()),

time: 209 us -> 135 us (0.65)
  Pallas kernels: 0 us -> 125 us
  waiting for transfers between devices: 95.6 us -> 0 us
  blocking collectives: 41.1 us -> 0 us
  starting transfers between devices: 33.9 us -> 0 us
  local copies, waits for them, and re-layouts: 25 us -> 5.35 us
  matrix products: 5.25 us -> 0 us
    pallas_call x0 -> x1, Pallas kernels: none -> 125 us  [fused(): pl.pallas_call(functools.partial(kernel, line, groups), out_shape=(jax.Sh...]
    all_to_all x4 -> x0, waiting for transfers between devices: 95.6 us -> none  [the longest x1 41 us: local(): lax.all_to_all(block_grad, 'shard', split_axis=3, concat_axis=0, tiled=True)]
    psum x1 -> x0, blocking collectives: 41.1 us -> none  [local(): totals = lax.psum((jnp.sum(row_loss), temp_part), ('dp', 'shard'))]
    all_to_all x4 -> x0, starting transfers between devices: 33.9 us -> none  [the longest x1 11.3 us: local(): lax.all_to_all(block_grad, 'shard', split_axis=3, concat_axis=0, tiled=True)]
    reshape x3 -> x0, local copies, waits for them, and re-layouts: 7.23 us -> none  [the longest x1 4.96 us: local(): returned.reshape(shard_count * listed, row_count * col_piece)]
    dot_general x4 -> x0, matrix products: 5.25 us -> none  [the longest x1 3.31 us: local(): jnp.einsum('mqk,mkd->qd', weights, key_rows, preferred_element_type=jnp.f...]
    all_to_all x3 -> x0, local copies, waits for them, and re-layouts: 5.16 us -> none  [the longest x2 5.03 us: local(): lax.all_to_all(block_grad, 'shard', split_axis=3, concat_axis=0, tiled=True)]
    gather x2 -> x0, local copies, waits for them, and re-layouts: 4.39 us -> none  [the longest x1 2.37 us: local(): row_loss = row_peak + jnp.log(exp_total) - jnp.diagonal(logits[0])]
  transfers between devices with their start and end apart: 4 -> 0, of which waited for: 3 -> 0; matrix products, arithmetic and copies ran while one was open for 4% -> 0% of each run, Pallas kernels for 0% -> 0%
where the time goes in v1:
time: 135 us
  Pallas kernels  125 us (93%)
  local copies, waits for them, and re-layouts  5.35 us (4%)
  between operations  4.86 us (4%)
    pallas_call x1, Pallas kernels, fused(): pl.pallas_call(functools.partial(kernel, line, groups), out_shape=(jax.Sh...  125 us
    unnamed x5, local copies, waits for them, and re-layouts  4.08 us

profile of v1, /device:TPU:0, one launch (start us, length us, event | category | flops | bytes accessed | tf_op | source)
XLA Modules:
  0.0 135.1 jit_solution(14916747838428688538)
XLA Ops:
  0.6 1.4 %copy.8.lists = s32[16,4]{1,0:T(8,128)} copy(s32[16,4]{0,1:T(4,128)} %param.6) | data formatting | bytes 512 | tf_op args[2]
  2.6 124.9 %shard_map.75 = (bf16[256,1024]{1,0:T(8,128)(2,1)}, bf16[256,1024]{1,0:T(8,128)(2,1)}, f32[8,128]{1,0:T(8,128)}) custom-call(bf16[256,1024]{1,0:T(8,128)(2,1)} %q_in.1, bf16[256,1024]{1,0:T(8,128)(2,1)} %p_in.1, s32[16,4]{1,0:T(8,128)} %copy.8.lists, f32[1]{0:T(128)} %bitcast.3.temp), custom_call_target="tpu_custom_call" | custom-call | tf_op jit(solution)/shard_map/pallas_call | solution.py:398
  127.5 1.3 fusion
  130.1 0.0 copy-start
  130.1 1.9 %copy.12 = bf16[256,1024]{1,0:T(8,128)(2,1)} copy(bf16[256,1024]{1,0:T(8,128)(2,1)} %get-tuple-element.16) | data formatting | bytes 1048576
  132.0 0.0 copy-done
  132.1 0.8 copy.13
Async XLA Ops:
  130.1 1.9 %copy-start = (bf16[256,1024]{1,0:T(8,128)(2,1)S(1)}, bf16[256,1024]{1,0:T(8,128)(2,1)}, u32[]{:S(2)}) copy-start(bf16[256,1024]{1,0:T(8,128)(2,1)} %get-tuple-element.17) | copy-start | bytes 1572868

commit v2 on v1

--- a/solution.py
+++ b/solution.py
@@ -57,7 +57,7 @@
         bit *= 2
 
     mine = z * 2 + k
-    own_p = pltpu.make_async_copy(p_in, pcol.at[mine], loc_sem.at[0])
+    own_p = pltpu.make_async_copy(p_in, pcol.at[pl.ds(mine * rows, rows)], loc_sem.at[0])
     own_q = pltpu.make_async_copy(q_in, qcat.at[pl.ds(x * rows, rows)], loc_sem.at[1])
     own_p.start()
     own_q.start()
@@ -84,10 +84,12 @@
 
     def p_copy(zz, sems, d):
         slot = zz * 2 + k
-        return remote(pcol.at[slot], pcol.at[slot], sems.at[zz], p_recv.at[slot], d)
+        span = pcol.at[pl.ds(slot * rows, rows)]
+        return remote(span, span, sems.at[zz], p_recv.at[slot], d)
 
     def p_wait(slot):
-        remote(pcol.at[slot], pcol.at[slot], p_core.at[0], p_recv.at[slot], core).wait_recv()
+        span = pcol.at[pl.ds(slot * rows, rows)]
+        remote(span, span, p_core.at[0], p_recv.at[slot], core).wait_recv()
 
     my_rows = pl.ds(x * rows, rows)
     q_copy = remote(qcat.at[my_rows], qcat.at[my_rows], q_sems.at[0], q_sems.at[1], mate)
@@ -134,7 +136,7 @@
         ident = block_of(slot)
         live = per_lane(ident, 0, listed) > 0
         pos = per_lane(ident, 0, 1) > 0
-        s = dot(pcol[slot], qcat[...], NT) * inv_temp
+        s = dot(pcol[pl.ds(slot * rows, rows)], qcat[...], NT) * inv_temp
         s = jnp.where(live, s, LOW)
         m_old = stat[0:1, :]
         m_new = jnp.maximum(m_old, jnp.max(s, axis=0, keepdims=True))
@@ -148,6 +150,11 @@
         stat[3:4, :] = stat[3:4, :] + jnp.where(pos, diag, 0.0)
         mrec[slot] = jnp.broadcast_to(m_new, (8, 2 * rows))
 
+    def take_pair(zz):
+        consume(zz * 2 + k)
+        p_wait(zz * 2 + 1 - k)
+        consume(zz * 2 + 1 - k)
+
     q_wait.wait_recv()
 
     @pl.loop(0, line - 1)
@@ -181,17 +188,17 @@
             p_wait(z * 2 + 1 - k)
             consume(z * 2 + 1 - k)
 
+        @pl.when((s > 0) & (from_l + 1 >= 0) & (from_r - 1 < line))
+        def _():
+            take_pair(from_r - 1)
+
         @pl.when(from_l >= 0)
         def _():
-            consume(from_l * 2 + k)
-            p_wait(from_l * 2 + 1 - k)
-            consume(from_l * 2 + 1 - k)
-
-        @pl.when(from_r < line)
-        def _():
-            consume(from_r * 2 + k)
-            p_wait(from_r * 2 + 1 - k)
-            consume(from_r * 2 + 1 - k)
+            take_pair(from_l)
+
+        @pl.when((from_r < line) & (from_l < 0))
+        def _():
+            take_pair(from_r)
 
     st_copy = remote(stat, stat_in, st_sems.at[0], st_sems.at[1], mate)
     st_copy.start()
@@ -207,7 +214,7 @@
         scale = jnp.exp(mrec[slot][0:1, :] - peak) * inv_total
         target = jnp.where(jnp.logical_and(eye, pos), 1.0, 0.0)
         w = (ebuf[slot] * scale - target).astype(jnp.bfloat16)
-        wbuf[slot] = w
+        wbuf[pl.ds(slot * rows, rows)] = w
         return w
 
     def p_grad(slot):
@@ -266,10 +273,26 @@
     take(z)
 
     def q_part(start):
-        part = jnp.zeros((rows, q_in.shape[1]), jnp.float32)
-        for c in range(2 * line):
-            part = part + dot(wbuf[c, :, pl.ds(start, rows)], pcol[c], TN)
-        return part * inv_temp
+        return dot(wbuf[:, pl.ds(start, rows)], pcol[...], TN) * inv_temp
+
+    def pass_on(t):
+        dr = line - 1 + z - t
+        dl = t - (line - 1 - z)
+
+        @pl.when((dr > z) & (dr < line) & has_l)
+        def _():
+            r_copy(dr).wait_recv()
+            zsend[dr] = (own[dr] + zin_r[dr].astype(jnp.float32)).astype(jnp.bfloat16)
+            r_copy(dr).start()
+
+        @pl.when((dl < z) & (dl >= 0) & has_r)
+        def _():
+            l_copy(dl).wait_recv()
+            zsend[dl] = (own[dl] + zin_l[dl].astype(jnp.float32)).astype(jnp.bfloat16)
+            l_copy(dl).start()
+
+    if line > 2:
+        pass_on(1)
 
     @pl.when(x == 0)
     def _():
@@ -282,9 +305,21 @@
     g_copy = remote(qsend, qrecv, g_sems.at[0], g_sems.at[1], mate)
     g_copy.start()
 
-    owner = (lane >= x * rows) & (lane < x * rows + rows)
+    @pl.loop(2, line - 1)
+    def _(t):
+        pass_on(t)
+
+    @pl.when(x == 0)
+    def _():
+        qg_out[...] = q_part(0).astype(jnp.bfloat16)
+
+    @pl.when(x == 1)
+    def _():
+        qg_out[...] = q_part(rows).astype(jnp.bfloat16)
+
+    own_lane = (lane >= x * rows) & (lane < x * rows + rows)
     diag = stat[3:4, :]
-    loss = jnp.where(owner, peak + jnp.log(total), 0.0) - diag
+    loss = jnp.where(own_lane, peak + jnp.log(total), 0.0) - diag
     grad = stat[2:3, :] * (jnp.exp(m_loc - peak) * inv_total) - diag
     loss = jnp.sum(loss, axis=1, keepdims=True)
     grad = jnp.sum(grad, axis=1, keepdims=True) / inv_temp
@@ -299,31 +334,6 @@
         a_copies.append(copy)
     tot_out[...] = acc[len(pairs)]
 
-    @pl.when(x == 0)
-    def _():
-        qg_out[...] = q_part(0).astype(jnp.bfloat16)
-
-    @pl.when(x == 1)
-    def _():
-        qg_out[...] = q_part(rows).astype(jnp.bfloat16)
-
-    @pl.loop(0, line - 1)
-    def _(s):
-        dr = line - 1 - s
-        dl = s
-
-        @pl.when((dr > z) & has_l)
-        def _():
-            r_copy(dr).wait_recv()
-            zsend[dr] = (own[dr] + zin_r[dr].astype(jnp.float32)).astype(jnp.bfloat16)
-            r_copy(dr).start()
-
-        @pl.when((dl < z) & has_r)
-        def _():
-            l_copy(dl).wait_recv()
-            zsend[dl] = (own[dl] + zin_l[dl].astype(jnp.float32)).astype(jnp.bfloat16)
-            l_copy(dl).start()
-
     g_copy.wait_recv()
     qg_out[...] = (qg_out[...].astype(jnp.float32) + qrecv[...].astype(jnp.float32)).astype(jnp.bfloat16)
 
@@ -374,10 +384,10 @@
     block = (rows, width)
     vm, dma = pltpu.VMEM, pltpu.SemaphoreType.DMA
     scratch = [
-        vm((2 * line,) + block, bf),
+        vm((2 * line * rows, width), bf),
         vm((2 * rows, width), bf),
         vm((2 * line, rows, 2 * rows), f32),
-        vm((2 * line, rows, 2 * rows), bf),
+        vm((2 * line * rows, 2 * rows), bf),
         vm((2 * line, 8, 2 * rows), f32),
         vm((8, 2 * rows), f32),
         vm((8, 2 * rows), f32),

time: 135 us -> 103 us (0.76)
  Pallas kernels: 125 us -> 92.1 us
    pallas_call x1, Pallas kernels: 125 us -> 92.1 us  [fused(): pl.pallas_call(functools.partial(kernel, line, groups), out_shape=(jax.Sh...]
where the time goes in v2:
time: 103 us; the launch traced here: 102 us
  Pallas kernels  92.1 us (89%)
  local copies, waits for them, and re-layouts  5.35 us (5%)
  between operations  4.86 us (5%)
    pallas_call x1, Pallas kernels, fused(): pl.pallas_call(functools.partial(kernel, line, groups), out_shape=(jax.Sh...  92.1 us
    unnamed x5, local copies, waits for them, and re-layouts  4.08 us

profile of v2, /device:TPU:0, one launch (start us, length us, event | category | flops | bytes accessed | tf_op | source)
XLA Modules:
  0.0 102.3 jit_solution(4267602521342598334)
XLA Ops:
  0.6 1.4 %copy.8.lists = s32[16,4]{1,0:T(8,128)} copy(s32[16,4]{0,1:T(4,128)} %param.6) | data formatting | bytes 512 | tf_op args[2]
  2.6 92.1 %shard_map.75 = (bf16[256,1024]{1,0:T(8,128)(2,1)}, bf16[256,1024]{1,0:T(8,128)(2,1)}, f32[8,128]{1,0:T(8,128)}) custom-call(bf16[256,1024]{1,0:T(8,128)(2,1)} %q_in.1, bf16[256,1024]{1,0:T(8,128)(2,1)} %p_in.1, s32[16,4]{1,0:T(8,128)} %copy.8.lists, f32[1]{0:T(128)} %bitcast.3.temp), custom_call_target="tpu_custom_call" | custom-call | tf_op jit(solution)/shard_map/pallas_call | solution.py:408
  94.8 1.3 %fusion = (f32[1,1]{1,0:T(1,128)}, f32[1,1]{1,0:T(1,128)}) fusion(f32[8,128]{1,0:T(8,128)} %get-tuple-element.9), kind=kLoop, calls=%fused_computation | loop fusion | bytes 16 | tf_op jit(solution)/shard_map/slice | solution.py:428
  97.3 0.0 copy-start
  97.3 1.9 %copy.12 = bf16[256,1024]{1,0:T(8,128)(2,1)} copy(bf16[256,1024]{1,0:T(8,128)(2,1)} %get-tuple-element.16) | data formatting | bytes 1048576
  99.3 0.0 copy-done
  99.3 0.8 copy.13
Async XLA Ops:
  97.3 1.9 %copy-start = (bf16[256,1024]{1,0:T(8,128)(2,1)S(1)}, bf16[256,1024]{1,0:T(8,128)(2,1)}, u32[]{:S(2)}) copy-start(bf16[256,1024]{1,0:T(8,128)(2,1)} %get-tuple-element.17) | copy-start | bytes 1572868

commit v3 on v1

--- a/solution.py
+++ b/solution.py
@@ -12,6 +12,7 @@
 NT = (((1,), (1,)), ((), ()))
 TN = (((0,), (0,)), ((), ()))
 NN = (((1,), (0,)), ((), ()))
+CUT = 2
 
 
 def dot(a, b, dims):
@@ -25,6 +26,7 @@
            c_send, c_recv, r_send, r_recv, l_send, l_recv, g_sems, a_send, a_recv):
     rows = q_in.shape[0]
     listed = lists.shape[1]
+    half = rows // CUT
     dp = lax.axis_index("dp")
     me = lax.axis_index("shard")
     k = lax.rem(me, 2)
@@ -57,7 +59,7 @@
         bit *= 2
 
     mine = z * 2 + k
-    own_p = pltpu.make_async_copy(p_in, pcol.at[mine], loc_sem.at[0])
+    own_p = pltpu.make_async_copy(p_in, pcol.at[pl.ds(mine * rows, rows)], loc_sem.at[0])
     own_q = pltpu.make_async_copy(q_in, qcat.at[pl.ds(x * rows, rows)], loc_sem.at[1])
     own_p.start()
     own_q.start()
@@ -82,12 +84,17 @@
             src_ref=src, dst_ref=dst, send_sem=send, recv_sem=recv,
             device_id=d, device_id_type=MESH)
 
-    def p_copy(zz, sems, d):
+    def p_span(slot, c):
+        return pcol.at[pl.ds(slot * rows + c * half, half)]
+
+    def p_copy(zz, c, sems, d):
         slot = zz * 2 + k
-        return remote(pcol.at[slot], pcol.at[slot], sems.at[zz], p_recv.at[slot], d)
-
-    def p_wait(slot):
-        remote(pcol.at[slot], pcol.at[slot], p_core.at[0], p_recv.at[slot], core).wait_recv()
+        span = p_span(slot, c)
+        return remote(span, span, sems.at[zz * CUT + c], p_recv.at[slot * CUT + c], d)
+
+    def p_wait(slot, c):
+        span = p_span(slot, c)
+        remote(span, span, p_core.at[0], p_recv.at[slot * CUT + c], core).wait_recv()
 
     my_rows = pl.ds(x * rows, rows)
     q_copy = remote(qcat.at[my_rows], qcat.at[my_rows], q_sems.at[0], q_sems.at[1], mate)
@@ -96,22 +103,24 @@
 
     own_p.wait()
 
-    @pl.when(has_r)
-    def _():
-        p_copy(z, p_right, right).start()
-
-    @pl.when(has_l)
-    def _():
-        p_copy(z, p_left, left).start()
+    for c in range(CUT):
+        @pl.when(has_r)
+        def _(c=c):
+            p_copy(z, c, p_right, right).start()
+
+        @pl.when(has_l)
+        def _(c=c):
+            p_copy(z, c, p_left, left).start()
 
     own_q.wait()
     q_copy.start()
-    p_copy(z, p_core, core).start()
+    for c in range(CUT):
+        p_copy(z, c, p_core, core).start()
 
     lane = lax.broadcasted_iota(jnp.int32, (1, 2 * rows), 1)
-    jj = lax.broadcasted_iota(jnp.int32, (rows, 2 * rows), 0)
-    ii = lax.broadcasted_iota(jnp.int32, (rows, 2 * rows), 1)
-    eye = jj == jnp.where(ii < rows, ii, ii - rows)
+    jj = lax.broadcasted_iota(jnp.int32, (half, 2 * rows), 0)
+    ii = lax.broadcasted_iota(jnp.int32, (half, 2 * rows), 1)
+    ahead = jnp.where(ii < rows, ii, ii - rows) - jj
     inv_temp = temp[0]
     row_a = z * 4 + k
     row_b = z * 4 + 2 + k
@@ -130,68 +139,74 @@
     stat[0:1, :] = jnp.full((1, 2 * rows), LOW, jnp.float32)
     stat[1:8, :] = jnp.zeros((7, 2 * rows), jnp.float32)
 
-    def consume(slot):
+    def consume(slot, c):
+        part = slot * CUT + c
         ident = block_of(slot)
         live = per_lane(ident, 0, listed) > 0
         pos = per_lane(ident, 0, 1) > 0
-        s = dot(pcol[slot], qcat[...], NT) * inv_temp
+        s = dot(pcol[pl.ds(slot * rows + c * half, half)], qcat[...], NT) * inv_temp
         s = jnp.where(live, s, LOW)
         m_old = stat[0:1, :]
         m_new = jnp.maximum(m_old, jnp.max(s, axis=0, keepdims=True))
         e = jnp.exp(s - m_new)
-        ebuf[slot] = e
+        ebuf[part] = e
         scale = jnp.exp(m_old - m_new)
         stat[0:1, :] = m_new
         stat[1:2, :] = stat[1:2, :] * scale + jnp.sum(e, axis=0, keepdims=True)
         stat[2:3, :] = stat[2:3, :] * scale + jnp.sum(e * s, axis=0, keepdims=True)
-        diag = jnp.sum(jnp.where(eye, s, 0.0), axis=0, keepdims=True)
+        diag = jnp.sum(jnp.where(ahead == c * half, s, 0.0), axis=0, keepdims=True)
         stat[3:4, :] = stat[3:4, :] + jnp.where(pos, diag, 0.0)
-        mrec[slot] = jnp.broadcast_to(m_new, (8, 2 * rows))
+        mrec[part] = jnp.broadcast_to(m_new, (8, 2 * rows))
+
+    def take_pair(zz, c):
+        consume(zz * 2 + k, c)
+        p_wait(zz * 2 + 1 - k, c)
+        consume(zz * 2 + 1 - k, c)
 
     q_wait.wait_recv()
 
-    @pl.loop(0, line - 1)
-    def _(s):
+    @pl.loop(0, (line - 1) * CUT)
+    def _(t):
+        s = t // CUT
+        c = lax.rem(t, CUT)
         from_l = z - 1 - s
         from_r = z + 1 + s
 
         @pl.when(from_l >= 0)
         def _():
-            p_wait(from_l * 2 + k)
+            p_wait(from_l * 2 + k, c)
 
             @pl.when(has_r)
             def _():
-                p_copy(from_l, p_right, right).start()
-
-            p_copy(from_l, p_core, core).start()
+                p_copy(from_l, c, p_right, right).start()
+
+            p_copy(from_l, c, p_core, core).start()
 
         @pl.when(from_r < line)
         def _():
-            p_wait(from_r * 2 + k)
+            p_wait(from_r * 2 + k, c)
 
             @pl.when(has_l)
             def _():
-                p_copy(from_r, p_left, left).start()
-
-            p_copy(from_r, p_core, core).start()
+                p_copy(from_r, c, p_left, left).start()
+
+            p_copy(from_r, c, p_core, core).start()
 
         @pl.when(s == 0)
         def _():
-            consume(mine)
-            p_wait(z * 2 + 1 - k)
-            consume(z * 2 + 1 - k)
+            take_pair(z, c)
+
+        @pl.when((s > 0) & (from_l + 1 >= 0) & (from_r - 1 < line))
+        def _():
+            take_pair(from_r - 1, c)
 
         @pl.when(from_l >= 0)
         def _():
-            consume(from_l * 2 + k)
-            p_wait(from_l * 2 + 1 - k)
-            consume(from_l * 2 + 1 - k)
-
-        @pl.when(from_r < line)
-        def _():
-            consume(from_r * 2 + k)
-            p_wait(from_r * 2 + 1 - k)
-            consume(from_r * 2 + 1 - k)
+            take_pair(from_l, c)
+
+        @pl.when((from_r < line) & (from_l < 0))
+        def _():
+            take_pair(from_r, c)
 
     st_copy = remote(stat, stat_in, st_sems.at[0], st_sems.at[1], mate)
     st_copy.start()
@@ -204,11 +219,13 @@
 
     def make_w(slot):
         pos = per_lane(block_of(slot), 0, 1) > 0
-        scale = jnp.exp(mrec[slot][0:1, :] - peak) * inv_total
-        target = jnp.where(jnp.logical_and(eye, pos), 1.0, 0.0)
-        w = (ebuf[slot] * scale - target).astype(jnp.bfloat16)
-        wbuf[slot] = w
-        return w
+        for c in range(CUT):
+            part = slot * CUT + c
+            scale = jnp.exp(mrec[part][0:1, :] - peak) * inv_total
+            target = jnp.where(jnp.logical_and(ahead == c * half, pos), 1.0, 0.0)
+            w = (ebuf[part] * scale - target).astype(jnp.bfloat16)
+            wbuf[pl.ds(slot * rows + c * half, half)] = w
+        return wbuf[pl.ds(slot * rows, rows)]
 
     def p_grad(slot):
         return dot(make_w(slot), qcat[...], NN) * inv_temp
@@ -216,11 +233,16 @@
     def c_copy(d):
         return remote(psend.at[d], chip_in.at[d], c_send.at[d], c_recv.at[d], core)
 
-    def r_copy(d):
-        return remote(zsend.at[d], zin_r.at[d], r_send.at[d], r_recv.at[d], right)
-
-    def l_copy(d):
-        return remote(zsend.at[d], zin_l.at[d], l_send.at[d], l_recv.at[d], left)
+    def cut(ref, d, c):
+        return ref.at[d, pl.ds(c * half, half)]
+
+    def r_copy(d, c):
+        i = d * CUT + c
+        return remote(cut(zsend, d, c), cut(zin_r, d, c), r_send.at[i], r_recv.at[i], right)
+
+    def l_copy(d, c):
+        i = d * CUT + c
+        return remote(cut(zsend, d, c), cut(zin_l, d, c), l_send.at[i], l_recv.at[i], left)
 
     def give(d):
         psend[d] = p_grad(d * 2 + 1 - k).astype(jnp.bfloat16)
@@ -251,7 +273,8 @@
             @pl.when(z == 0)
             def _():
                 zsend[dr] = own[dr].astype(jnp.bfloat16)
-                r_copy(dr).start()
+                for c in range(CUT):
+                    r_copy(dr, c).start()
 
         @pl.when(dl < z)
         def _():
@@ -260,16 +283,41 @@
             @pl.when(z == line - 1)
             def _():
                 zsend[dl] = own[dl].astype(jnp.bfloat16)
-                l_copy(dl).start()
+                for c in range(CUT):
+                    l_copy(dl, c).start()
 
     give(z)
     take(z)
 
     def q_part(start):
-        part = jnp.zeros((rows, q_in.shape[1]), jnp.float32)
-        for c in range(2 * line):
-            part = part + dot(wbuf[c, :, pl.ds(start, rows)], pcol[c], TN)
-        return part * inv_temp
+        return dot(wbuf[:, pl.ds(start, rows)], pcol[...], TN) * inv_temp
+
+    def pass_on(t):
+        n = jnp.maximum(t - z, 0)
+        dr = line - 1 - n // CUT
+        cr = lax.rem(n, CUT)
+
+        @pl.when((t >= z) & (dr > z) & has_l)
+        def _():
+            r_copy(dr, cr).wait_recv()
+            here = pl.ds(cr * half, half)
+            zsend[dr, here] = (own[dr, here] + zin_r[dr, here].astype(jnp.float32)).astype(jnp.bfloat16)
+            r_copy(dr, cr).start()
+
+        n = jnp.maximum(t - (line - 1 - z), 0)
+        dl = n // CUT
+        cl = lax.rem(n, CUT)
+
+        @pl.when((t >= line - 1 - z) & (dl < z) & has_r)
+        def _():
+            l_copy(dl, cl).wait_recv()
+            here = pl.ds(cl * half, half)
+            zsend[dl, here] = (own[dl, here] + zin_l[dl, here].astype(jnp.float32)).astype(jnp.bfloat16)
+            l_copy(dl, cl).start()
+
+    last = (line - 2) * CUT
+    if last >= 1:
+        pass_on(1)
 
     @pl.when(x == 0)
     def _():
@@ -282,22 +330,26 @@
     g_copy = remote(qsend, qrecv, g_sems.at[0], g_sems.at[1], mate)
     g_copy.start()
 
-    owner = (lane >= x * rows) & (lane < x * rows + rows)
+    own_lane = (lane >= x * rows) & (lane < x * rows + rows)
     diag = stat[3:4, :]
-    loss = jnp.where(owner, peak + jnp.log(total), 0.0) - diag
+    loss = jnp.where(own_lane, peak + jnp.log(total), 0.0) - diag
     grad = stat[2:3, :] * (jnp.exp(m_loc - peak) * inv_total) - diag
     loss = jnp.sum(loss, axis=1, keepdims=True)
     grad = jnp.sum(grad, axis=1, keepdims=True) / inv_temp
     tile_row = lax.broadcasted_iota(jnp.int32, (8, 128), 0)
     acc[0] = jnp.where(tile_row == 0, loss, grad)
     a_copies = []
-    for i, d in enumerate(pairs):
-        copy = remote(acc.at[i], acc_in.at[i], a_send.at[i], a_recv.at[i], d)
+
+    def add_up(i):
+        copy = remote(acc.at[i], acc_in.at[i], a_send.at[i], a_recv.at[i], pairs[i])
         copy.start()
         copy.wait_recv()
         acc[i + 1] = acc[i] + acc_in[i]
         a_copies.append(copy)
-    tot_out[...] = acc[len(pairs)]
+
+    add_up(0)
+    if last >= 2:
+        pass_on(2)
 
     @pl.when(x == 0)
     def _():
@@ -307,37 +359,33 @@
     def _():
         qg_out[...] = q_part(rows).astype(jnp.bfloat16)
 
-    @pl.loop(0, line - 1)
-    def _(s):
-        dr = line - 1 - s
-        dl = s
-
-        @pl.when((dr > z) & has_l)
-        def _():
-            r_copy(dr).wait_recv()
-            zsend[dr] = (own[dr] + zin_r[dr].astype(jnp.float32)).astype(jnp.bfloat16)
-            r_copy(dr).start()
-
-        @pl.when((dl < z) & has_r)
-        def _():
-            l_copy(dl).wait_recv()
-            zsend[dl] = (own[dl] + zin_l[dl].astype(jnp.float32)).astype(jnp.bfloat16)
-            l_copy(dl).start()
+    add_up(1)
+
+    @pl.loop(3, last + 1)
+    def _(t):
+        pass_on(t)
+
+    for i in range(2, len(pairs)):
+        add_up(i)
+    tot_out[...] = acc[len(pairs)]
 
     g_copy.wait_recv()
     qg_out[...] = (qg_out[...].astype(jnp.float32) + qrecv[...].astype(jnp.float32)).astype(jnp.bfloat16)
 
-    @pl.when(has_l)
-    def _():
-        r_copy(z).wait_recv()
-        own[z] = own[z] + zin_r[z].astype(jnp.float32)
-
-    @pl.when(has_r)
-    def _():
-        l_copy(z).wait_recv()
-        own[z] = own[z] + zin_l[z].astype(jnp.float32)
-
-    pg_out[...] = own[z].astype(jnp.bfloat16)
+    for c in range(CUT):
+        here = pl.ds(c * half, half)
+
+        @pl.when(has_l)
+        def _(c=c, here=here):
+            r_copy(z, c).wait_recv()
+            own[z, here] = own[z, here] + zin_r[z, here].astype(jnp.float32)
+
+        @pl.when(has_r)
+        def _(c=c, here=here):
+            l_copy(z, c).wait_recv()
+            own[z, here] = own[z, here] + zin_l[z, here].astype(jnp.float32)
+
+        pg_out[here] = own[z, here].astype(jnp.bfloat16)
 
     q_copy.wait_send()
     st_copy.wait_send()
@@ -347,24 +395,25 @@
 
     @pl.loop(0, line)
     def _(d):
-        p_copy(d, p_core, core).wait_send()
         c_copy(d).wait_send()
-
-        @pl.when((d <= z) & has_r)
-        def _():
-            p_copy(d, p_right, right).wait_send()
-
-        @pl.when((d >= z) & has_l)
-        def _():
-            p_copy(d, p_left, left).wait_send()
-
-        @pl.when(d > z)
-        def _():
-            r_copy(d).wait_send()
-
-        @pl.when(d < z)
-        def _():
-            l_copy(d).wait_send()
+        for c in range(CUT):
+            p_copy(d, c, p_core, core).wait_send()
+
+            @pl.when((d <= z) & has_r)
+            def _(c=c):
+                p_copy(d, c, p_right, right).wait_send()
+
+            @pl.when((d >= z) & has_l)
+            def _(c=c):
+                p_copy(d, c, p_left, left).wait_send()
+
+            @pl.when(d > z)
+            def _(c=c):
+                r_copy(d, c).wait_send()
+
+            @pl.when(d < z)
+            def _(c=c):
+                l_copy(d, c).wait_send()
 
 
 def fused(line, groups, queries, passages, block_lists, inv_temp):
@@ -374,11 +423,11 @@
     block = (rows, width)
     vm, dma = pltpu.VMEM, pltpu.SemaphoreType.DMA
     scratch = [
-        vm((2 * line,) + block, bf),
+        vm((2 * line * rows, width), bf),
         vm((2 * rows, width), bf),
-        vm((2 * line, rows, 2 * rows), f32),
-        vm((2 * line, rows, 2 * rows), bf),
-        vm((2 * line, 8, 2 * rows), f32),
+        vm((2 * line * CUT, rows // CUT, 2 * rows), f32),
+        vm((2 * line * rows, 2 * rows), bf),
+        vm((2 * line * CUT, 8, 2 * rows), f32),
         vm((8, 2 * rows), f32),
         vm((8, 2 * rows), f32),
         vm((line,) + block, bf),
@@ -391,8 +440,9 @@
         vm(block, bf),
         vm((stages + 1, 8, 128), f32),
         vm((stages, 8, 128), f32),
-        dma((2,)), dma((2,)), dma((2 * line,)), dma((line,)), dma((line,)), dma((line,)), dma((2,)),
-        dma((line,)), dma((line,)), dma((line,)), dma((line,)), dma((line,)), dma((line,)),
+        dma((2,)), dma((2,)), dma((2 * line * CUT,)), dma((line * CUT,)), dma((line * CUT,)),
+        dma((line * CUT,)), dma((2,)), dma((line,)), dma((line,)), dma((line * CUT,)),
+        dma((line * CUT,)), dma((line * CUT,)), dma((line * CUT,)),
         dma((2,)), dma((stages,)), dma((stages,)),
     ]
     query_grad, passage_grad, totals = pl.pallas_call(

time: 135 us -> 102 us (0.76)
  Pallas kernels: 125 us -> 91.6 us
    pallas_call x1, Pallas kernels: 125 us -> 91.6 us  [fused(): pl.pallas_call(functools.partial(kernel, line, groups), out_shape=(jax.Sh...]
where the time goes in v3:
time: 102 us
  Pallas kernels  91.6 us (90%)
  local copies, waits for them, and re-layouts  5.35 us (5%)
  between operations  4.86 us (5%)
    pallas_call x1, Pallas kernels, fused(): pl.pallas_call(functools.partial(kernel, line, groups), out_shape=(jax.Sh...  91.6 us
    unnamed x5, local copies, waits for them, and re-layouts  4.08 us

profile of v3, /device:TPU:0, one launch (start us, length us, event | category | flops | bytes accessed | tf_op | source)
XLA Modules:
  0.0 101.8 jit_solution(13849276200127348395)
XLA Ops:
  0.6 1.4 %copy.8.lists = s32[16,4]{1,0:T(8,128)} copy(s32[16,4]{0,1:T(4,128)} %param.6) | data formatting | bytes 512 | tf_op args[2]
  2.6 91.6 %shard_map.75 = (bf16[256,1024]{1,0:T(8,128)(2,1)}, bf16[256,1024]{1,0:T(8,128)(2,1)}, f32[8,128]{1,0:T(8,128)}) custom-call(bf16[256,1024]{1,0:T(8,128)(2,1)} %q_in.1, bf16[256,1024]{1,0:T(8,128)(2,1)} %p_in.1, s32[16,4]{1,0:T(8,128)} %copy.8.lists, f32[1]{0:T(128)} %bitcast.3.temp), custom_call_target="tpu_custom_call" | custom-call | tf_op jit(solution)/shard_map/pallas_call | solution.py:448
  94.2 1.3 %fusion = (f32[1,1]{1,0:T(1,128)}, f32[1,1]{1,0:T(1,128)}) fusion(f32[8,128]{1,0:T(8,128)} %get-tuple-element.9), kind=kLoop, calls=%fused_computation | loop fusion | bytes 16 | tf_op jit(solution)/shard_map/slice | solution.py:468
  96.8 0.0 copy-start
  96.8 1.9 %copy.12 = bf16[256,1024]{1,0:T(8,128)(2,1)} copy(bf16[256,1024]{1,0:T(8,128)(2,1)} %get-tuple-element.16) | data formatting | bytes 1048576
  98.7 0.0 copy-done
  98.7 0.8 copy.13
Async XLA Ops:
  96.8 1.9 %copy-start = (bf16[256,1024]{1,0:T(8,128)(2,1)S(1)}, bf16[256,1024]{1,0:T(8,128)(2,1)}, u32[]{:S(2)}) copy-start(bf16[256,1024]{1,0:T(8,128)(2,1)} %get-tuple-element.17) | copy-start | bytes 1572868

commit v4 on v3

--- a/solution.py
+++ b/solution.py
@@ -273,8 +273,11 @@
             @pl.when(z == 0)
             def _():
                 zsend[dr] = own[dr].astype(jnp.bfloat16)
-                for c in range(CUT):
-                    r_copy(dr, c).start()
+
+                @pl.when(s == 0)
+                def _():
+                    for c in range(CUT):
+                        r_copy(dr, c).start()
 
         @pl.when(dl < z)
         def _():
@@ -283,8 +286,11 @@
             @pl.when(z == line - 1)
             def _():
                 zsend[dl] = own[dl].astype(jnp.bfloat16)
-                for c in range(CUT):
-                    l_copy(dl, c).start()
+
+                @pl.when(s == 0)
+                def _():
+                    for c in range(CUT):
+                        l_copy(dl, c).start()
 
     give(z)
     take(z)
@@ -293,6 +299,20 @@
         return dot(wbuf[:, pl.ds(start, rows)], pcol[...], TN) * inv_temp
 
     def pass_on(t):
+        n = t - 1
+        ahead_of = n // CUT
+        cn = lax.rem(n, CUT)
+
+        @pl.when(z == 0)
+        def _():
+            r_copy(line - 1 - ahead_of, cn).wait_send()
+            r_copy(line - 2 - ahead_of, cn).start()
+
+        @pl.when(z == line - 1)
+        def _():
+            l_copy(ahead_of, cn).wait_send()
+            l_copy(ahead_of + 1, cn).start()
+
         n = jnp.maximum(t - z, 0)
         dr = line - 1 - n // CUT
         cr = lax.rem(n, CUT)
@@ -407,11 +427,11 @@
             def _(c=c):
                 p_copy(d, c, p_left, left).wait_send()
 
-            @pl.when(d > z)
+            @pl.when((d > z) & (has_l | (d == 1)))
             def _(c=c):
                 r_copy(d, c).wait_send()
 
-            @pl.when(d < z)
+            @pl.when((d < z) & (has_r | (d == line - 2)))
             def _(c=c):
                 l_copy(d, c).wait_send()
 

time: 102 us -> 102 us (level)
  no operation moved by 1% of the time
where the time goes in v4:
time: 102 us
  Pallas kernels  91.6 us (90%)
  local copies, waits for them, and re-layouts  5.35 us (5%)
  between operations  4.86 us (5%)
    pallas_call x1, Pallas kernels, fused(): pl.pallas_call(functools.partial(kernel, line, groups), out_shape=(jax.Sh...  91.6 us
    unnamed x5, local copies, waits for them, and re-layouts  4.08 us

profile of v4, /device:TPU:0, one launch (start us, length us, event | category | flops | bytes accessed | tf_op | source)
XLA Modules:
  0.0 101.8 jit_solution(916033549088722790)
XLA Ops:
  0.6 1.4 %copy.8.lists = s32[16,4]{1,0:T(8,128)} copy(s32[16,4]{0,1:T(4,128)} %param.6) | data formatting | bytes 512 | tf_op args[2]
  2.6 91.6 %shard_map.75 = (bf16[256,1024]{1,0:T(8,128)(2,1)}, bf16[256,1024]{1,0:T(8,128)(2,1)}, f32[8,128]{1,0:T(8,128)}) custom-call(bf16[256,1024]{1,0:T(8,128)(2,1)} %q_in.1, bf16[256,1024]{1,0:T(8,128)(2,1)} %p_in.1, s32[16,4]{1,0:T(8,128)} %copy.8.lists, f32[1]{0:T(128)} %bitcast.3.temp), custom_call_target="tpu_custom_call" | custom-call | tf_op jit(solution)/shard_map/pallas_call | solution.py:468
  94.2 1.3 %fusion = (f32[1,1]{1,0:T(1,128)}, f32[1,1]{1,0:T(1,128)}) fusion(f32[8,128]{1,0:T(8,128)} %get-tuple-element.9), kind=kLoop, calls=%fused_computation | loop fusion | bytes 16 | tf_op jit(solution)/shard_map/slice | solution.py:488
  96.8 0.0 copy-start
  96.8 1.9 %copy.12 = bf16[256,1024]{1,0:T(8,128)(2,1)} copy(bf16[256,1024]{1,0:T(8,128)(2,1)} %get-tuple-element.16) | data formatting | bytes 1048576
  98.7 0.0 copy-done
  98.7 0.8 copy.13
Async XLA Ops:
  96.8 1.9 %copy-start = (bf16[256,1024]{1,0:T(8,128)(2,1)S(1)}, bf16[256,1024]{1,0:T(8,128)(2,1)}, u32[]{:S(2)}) copy-start(bf16[256,1024]{1,0:T(8,128)(2,1)} %get-tuple-element.17) | copy-start | bytes 1572868

commit v5 on v4

--- a/solution.py
+++ b/solution.py
@@ -20,13 +20,14 @@
 
 
 def kernel(line, groups, q_in, p_in, lists, temp, qg_out, pg_out, tot_out,
-           pcol, qcat, ebuf, wbuf, mrec, stat, stat_in, chip_in, own, zin_r, zin_l,
+           pcol, qcat, qt, ebuf, wbuf, mrec, stat, stat_in, chip_in, own, zin_r, zin_l,
            zsend, psend, qsend, qrecv, acc, acc_in,
            loc_sem, q_sems, p_recv, p_right, p_left, p_core, st_sems,
            c_send, c_recv, r_send, r_recv, l_send, l_recv, g_sems, a_send, a_recv):
     rows = q_in.shape[0]
     listed = lists.shape[1]
     half = rows // CUT
+    wide = 2 * half
     dp = lax.axis_index("dp")
     me = lax.axis_index("shard")
     k = lax.rem(me, 2)
@@ -58,10 +59,17 @@
         far.append((other, me))
         bit *= 2
 
-    mine = z * 2 + k
-    own_p = pltpu.make_async_copy(p_in, pcol.at[pl.ds(mine * rows, rows)], loc_sem.at[0])
-    own_q = pltpu.make_async_copy(q_in, qcat.at[pl.ds(x * rows, rows)], loc_sem.at[1])
-    own_p.start()
+    own_p = [
+        pltpu.make_async_copy(
+            p_in.at[pl.ds(c * half, half)],
+            pcol.at[pl.ds(((z * CUT + c) * 2 + k) * half, half)],
+            loc_sem.at[c + 1],
+        )
+        for c in range(CUT)
+    ]
+    own_q = pltpu.make_async_copy(q_in, qcat.at[pl.ds(x * rows, rows)], loc_sem.at[0])
+    for copy in own_p:
+        copy.start()
     own_q.start()
 
     barrier = pltpu.get_barrier_semaphore()
@@ -84,24 +92,25 @@
             src_ref=src, dst_ref=dst, send_sem=send, recv_sem=recv,
             device_id=d, device_id_type=MESH)
 
-    def p_span(slot, c):
-        return pcol.at[pl.ds(slot * rows + c * half, half)]
+    def p_span(zz, c, kk):
+        return pcol.at[pl.ds(((zz * CUT + c) * 2 + kk) * half, half)]
 
     def p_copy(zz, c, sems, d):
-        slot = zz * 2 + k
-        span = p_span(slot, c)
-        return remote(span, span, sems.at[zz * CUT + c], p_recv.at[slot * CUT + c], d)
-
-    def p_wait(slot, c):
-        span = p_span(slot, c)
-        remote(span, span, p_core.at[0], p_recv.at[slot * CUT + c], core).wait_recv()
+        span = p_span(zz, c, k)
+        i = zz * CUT + c
+        return remote(span, span, sems.at[i], p_recv.at[i * 2 + k], d)
+
+    def p_wait(zz, c, kk):
+        span = p_span(zz, c, kk)
+        remote(span, span, p_core.at[0], p_recv.at[(zz * CUT + c) * 2 + kk], core).wait_recv()
 
     my_rows = pl.ds(x * rows, rows)
     q_copy = remote(qcat.at[my_rows], qcat.at[my_rows], q_sems.at[0], q_sems.at[1], mate)
     mate_rows = pl.ds((1 - x) * rows, rows)
     q_wait = remote(qcat.at[mate_rows], qcat.at[mate_rows], q_sems.at[0], q_sems.at[1], mate)
 
-    own_p.wait()
+    for copy in own_p:
+        copy.wait()
 
     for c in range(CUT):
         @pl.when(has_r)
@@ -116,6 +125,17 @@
     q_copy.start()
     for c in range(CUT):
         p_copy(z, c, p_core, core).start()
+
+    def turn(i):
+        qt[:, i * rows:(i + 1) * rows] = qcat[i * rows:(i + 1) * rows, :].T
+
+    @pl.when(x == 0)
+    def _():
+        turn(0)
+
+    @pl.when(x == 1)
+    def _():
+        turn(1)
 
     lane = lax.broadcasted_iota(jnp.int32, (1, 2 * rows), 1)
     jj = lax.broadcasted_iota(jnp.int32, (half, 2 * rows), 0)
@@ -133,19 +153,22 @@
             b = b + jnp.where(lists[row_b, m] == block_id, 1, 0)
         return jnp.where(lane < rows, a, b)
 
-    def block_of(slot):
-        return (slot // 2) * 4 + x * 2 + lax.rem(slot, 2)
+    def block_of(zz, kk):
+        return zz * 4 + x * 2 + kk
 
     stat[0:1, :] = jnp.full((1, 2 * rows), LOW, jnp.float32)
     stat[1:8, :] = jnp.zeros((7, 2 * rows), jnp.float32)
 
-    def consume(slot, c):
-        part = slot * CUT + c
-        ident = block_of(slot)
-        live = per_lane(ident, 0, listed) > 0
-        pos = per_lane(ident, 0, 1) > 0
-        s = dot(pcol[pl.ds(slot * rows + c * half, half)], qcat[...], NT) * inv_temp
-        s = jnp.where(live, s, LOW)
+    def consume(zz, c):
+        part = zz * CUT + c
+        live0 = per_lane(block_of(zz, 0), 0, listed) > 0
+        live1 = per_lane(block_of(zz, 1), 0, listed) > 0
+        pos0 = per_lane(block_of(zz, 0), 0, 1)
+        pos1 = per_lane(block_of(zz, 1), 0, 1)
+        s = dot(pcol[pl.ds(part * wide, wide)], qt[...], NN) * inv_temp
+        s0 = jnp.where(live0, s[:half], LOW)
+        s1 = jnp.where(live1, s[half:], LOW)
+        s = jnp.concatenate([s0, s1], axis=0)
         m_old = stat[0:1, :]
         m_new = jnp.maximum(m_old, jnp.max(s, axis=0, keepdims=True))
         e = jnp.exp(s - m_new)
@@ -154,16 +177,24 @@
         stat[0:1, :] = m_new
         stat[1:2, :] = stat[1:2, :] * scale + jnp.sum(e, axis=0, keepdims=True)
         stat[2:3, :] = stat[2:3, :] * scale + jnp.sum(e * s, axis=0, keepdims=True)
-        diag = jnp.sum(jnp.where(ahead == c * half, s, 0.0), axis=0, keepdims=True)
-        stat[3:4, :] = stat[3:4, :] + jnp.where(pos, diag, 0.0)
+        diag = jnp.where(ahead == c * half, jnp.where(pos0 > 0, s0, s1), 0.0)
+        diag = jnp.sum(diag, axis=0, keepdims=True)
+        stat[3:4, :] = stat[3:4, :] + jnp.where(pos0 + pos1 > 0, diag, 0.0)
         mrec[part] = jnp.broadcast_to(m_new, (8, 2 * rows))
 
     def take_pair(zz, c):
-        consume(zz * 2 + k, c)
-        p_wait(zz * 2 + 1 - k, c)
-        consume(zz * 2 + 1 - k, c)
+        p_wait(zz, c, 1 - k)
+        consume(zz, c)
 
     q_wait.wait_recv()
+
+    @pl.when(x == 0)
+    def _():
+        turn(1)
+
+    @pl.when(x == 1)
+    def _():
+        turn(0)
 
     @pl.loop(0, (line - 1) * CUT)
     def _(t):
@@ -174,7 +205,7 @@
 
         @pl.when(from_l >= 0)
         def _():
-            p_wait(from_l * 2 + k, c)
+            p_wait(from_l, c, k)
 
             @pl.when(has_r)
             def _():
@@ -184,7 +215,7 @@
 
         @pl.when(from_r < line)
         def _():
-            p_wait(from_r * 2 + k, c)
+            p_wait(from_r, c, k)
 
             @pl.when(has_l)
             def _():
@@ -217,80 +248,97 @@
     total = stat[1:2, :] * jnp.exp(m_loc - peak) + stat_in[1:2, :] * jnp.exp(m_in - peak)
     inv_total = 1.0 / total
 
-    def make_w(slot):
-        pos = per_lane(block_of(slot), 0, 1) > 0
+    own_lane = (lane >= x * rows) & (lane < x * rows + rows)
+    diag_row = stat[3:4, :]
+    loss = jnp.where(own_lane, peak + jnp.log(total), 0.0) - diag_row
+    grad = stat[2:3, :] * (jnp.exp(m_loc - peak) * inv_total) - diag_row
+    loss = jnp.sum(loss, axis=1, keepdims=True)
+    grad = jnp.sum(grad, axis=1, keepdims=True) / inv_temp
+    tile_row = lax.broadcasted_iota(jnp.int32, (8, 128), 0)
+    acc[0] = jnp.where(tile_row == 0, loss, grad)
+    a_copies = [
+        remote(acc.at[i], acc_in.at[i], a_send.at[i], a_recv.at[i], d) for i, d in enumerate(pairs)
+    ]
+    a_copies[0].start()
+
+    def add_up(i):
+        a_copies[i].wait_recv()
+        acc[i + 1] = acc[i] + acc_in[i]
+        if i + 1 < len(pairs):
+            a_copies[i + 1].start()
+
+    def p_grad(d):
+        pos0 = per_lane(block_of(d, 0), 0, 1) > 0
+        pos1 = per_lane(block_of(d, 1), 0, 1) > 0
         for c in range(CUT):
-            part = slot * CUT + c
+            part = d * CUT + c
             scale = jnp.exp(mrec[part][0:1, :] - peak) * inv_total
-            target = jnp.where(jnp.logical_and(ahead == c * half, pos), 1.0, 0.0)
-            w = (ebuf[part] * scale - target).astype(jnp.bfloat16)
-            wbuf[pl.ds(slot * rows + c * half, half)] = w
-        return wbuf[pl.ds(slot * rows, rows)]
-
-    def p_grad(slot):
-        return dot(make_w(slot), qcat[...], NN) * inv_temp
+            w = ebuf[part] * scale
+            w0 = w[:half] - jnp.where(jnp.logical_and(ahead == c * half, pos0), 1.0, 0.0)
+            w1 = w[half:] - jnp.where(jnp.logical_and(ahead == c * half, pos1), 1.0, 0.0)
+            wbuf[pl.ds(part * wide, half)] = w0.astype(jnp.bfloat16)
+            wbuf[pl.ds(part * wide + half, half)] = w1.astype(jnp.bfloat16)
+        g = dot(wbuf[pl.ds(d * CUT * wide, CUT * wide)], qcat[...], NN) * inv_temp
+        own[d] = g.reshape(2 * CUT, half, q_in.shape[1])
 
     def c_copy(d):
         return remote(psend.at[d], chip_in.at[d], c_send.at[d], c_recv.at[d], core)
 
-    def cut(ref, d, c):
-        return ref.at[d, pl.ds(c * half, half)]
-
     def r_copy(d, c):
         i = d * CUT + c
-        return remote(cut(zsend, d, c), cut(zin_r, d, c), r_send.at[i], r_recv.at[i], right)
+        return remote(zsend.at[d, c], zin_r.at[d, c], r_send.at[i], r_recv.at[i], right)
 
     def l_copy(d, c):
         i = d * CUT + c
-        return remote(cut(zsend, d, c), cut(zin_l, d, c), l_send.at[i], l_recv.at[i], left)
+        return remote(zsend.at[d, c], zin_l.at[d, c], l_send.at[i], l_recv.at[i], left)
 
     def give(d):
-        psend[d] = p_grad(d * 2 + 1 - k).astype(jnp.bfloat16)
+        p_grad(d)
+        for c in range(CUT):
+            psend[d, c] = own[d, c * 2 + 1 - k].astype(jnp.bfloat16)
         c_copy(d).start()
 
     def take(d):
-        own[d] = p_grad(d * 2 + k)
         c_copy(d).wait_recv()
-        own[d] = own[d] + chip_in[d].astype(jnp.float32)
-
-    @pl.loop(0, line - 1)
-    def _(s):
+        for c in range(CUT):
+            own[d, c * 2 + k] = own[d, c * 2 + k] + chip_in[d, c].astype(jnp.float32)
+
+    for s in range(line - 1):
         dr = line - 1 - s
         dl = s
 
         @pl.when(dr > z)
-        def _():
+        def _(dr=dr):
             give(dr)
 
         @pl.when(dl < z)
-        def _():
+        def _(dl=dl):
             give(dl)
 
         @pl.when(dr > z)
-        def _():
+        def _(s=s, dr=dr):
             take(dr)
 
             @pl.when(z == 0)
             def _():
-                zsend[dr] = own[dr].astype(jnp.bfloat16)
-
-                @pl.when(s == 0)
-                def _():
-                    for c in range(CUT):
+                for c in range(CUT):
+                    zsend[dr, c] = own[dr, c * 2 + k].astype(jnp.bfloat16)
+                    if s == 0:
                         r_copy(dr, c).start()
 
         @pl.when(dl < z)
-        def _():
+        def _(s=s, dl=dl):
             take(dl)
 
             @pl.when(z == line - 1)
             def _():
-                zsend[dl] = own[dl].astype(jnp.bfloat16)
-
-                @pl.when(s == 0)
-                def _():
-                    for c in range(CUT):
+                for c in range(CUT):
+                    zsend[dl, c] = own[dl, c * 2 + k].astype(jnp.bfloat16)
+                    if s == 0:
                         l_copy(dl, c).start()
+
+        if s < 2:
+            add_up(s)
 
     give(z)
     take(z)
@@ -320,8 +368,7 @@
         @pl.when((t >= z) & (dr > z) & has_l)
         def _():
             r_copy(dr, cr).wait_recv()
-            here = pl.ds(cr * half, half)
-            zsend[dr, here] = (own[dr, here] + zin_r[dr, here].astype(jnp.float32)).astype(jnp.bfloat16)
+            zsend[dr, cr] = (own[dr, cr * 2 + k] + zin_r[dr, cr].astype(jnp.float32)).astype(jnp.bfloat16)
             r_copy(dr, cr).start()
 
         n = jnp.maximum(t - (line - 1 - z), 0)
@@ -331,8 +378,7 @@
         @pl.when((t >= line - 1 - z) & (dl < z) & has_r)
         def _():
             l_copy(dl, cl).wait_recv()
-            here = pl.ds(cl * half, half)
-            zsend[dl, here] = (own[dl, here] + zin_l[dl, here].astype(jnp.float32)).astype(jnp.bfloat16)
+            zsend[dl, cl] = (own[dl, cl * 2 + k] + zin_l[dl, cl].astype(jnp.float32)).astype(jnp.bfloat16)
             l_copy(dl, cl).start()
 
     last = (line - 2) * CUT
@@ -350,24 +396,7 @@
     g_copy = remote(qsend, qrecv, g_sems.at[0], g_sems.at[1], mate)
     g_copy.start()
 
-    own_lane = (lane >= x * rows) & (lane < x * rows + rows)
-    diag = stat[3:4, :]
-    loss = jnp.where(own_lane, peak + jnp.log(total), 0.0) - diag
-    grad = stat[2:3, :] * (jnp.exp(m_loc - peak) * inv_total) - diag
-    loss = jnp.sum(loss, axis=1, keepdims=True)
-    grad = jnp.sum(grad, axis=1, keepdims=True) / inv_temp
-    tile_row = lax.broadcasted_iota(jnp.int32, (8, 128), 0)
-    acc[0] = jnp.where(tile_row == 0, loss, grad)
-    a_copies = []
-
-    def add_up(i):
-        copy = remote(acc.at[i], acc_in.at[i], a_send.at[i], a_recv.at[i], pairs[i])
-        copy.start()
-        copy.wait_recv()
-        acc[i + 1] = acc[i] + acc_in[i]
-        a_copies.append(copy)
-
-    add_up(0)
+    add_up(min(2, line - 1))
     if last >= 2:
         pass_on(2)
 
@@ -379,13 +408,13 @@
     def _():
         qg_out[...] = q_part(rows).astype(jnp.bfloat16)
 
-    add_up(1)
+    add_up(min(2, line - 1) + 1)
 
     @pl.loop(3, last + 1)
     def _(t):
         pass_on(t)
 
-    for i in range(2, len(pairs)):
+    for i in range(min(2, line - 1) + 2, len(pairs)):
         add_up(i)
     tot_out[...] = acc[len(pairs)]
 
@@ -393,19 +422,17 @@
     qg_out[...] = (qg_out[...].astype(jnp.float32) + qrecv[...].astype(jnp.float32)).astype(jnp.bfloat16)
 
     for c in range(CUT):
-        here = pl.ds(c * half, half)
-
         @pl.when(has_l)
-        def _(c=c, here=here):
+        def _(c=c):
             r_copy(z, c).wait_recv()
-            own[z, here] = own[z, here] + zin_r[z, here].astype(jnp.float32)
+            own[z, c * 2 + k] = own[z, c * 2 + k] + zin_r[z, c].astype(jnp.float32)
 
         @pl.when(has_r)
-        def _(c=c, here=here):
+        def _(c=c):
             l_copy(z, c).wait_recv()
-            own[z, here] = own[z, here] + zin_l[z, here].astype(jnp.float32)
-
-        pg_out[here] = own[z, here].astype(jnp.bfloat16)
+            own[z, c * 2 + k] = own[z, c * 2 + k] + zin_l[z, c].astype(jnp.float32)
+
+        pg_out[pl.ds(c * half, half)] = own[z, c * 2 + k].astype(jnp.bfloat16)
 
     q_copy.wait_send()
     st_copy.wait_send()
@@ -441,26 +468,29 @@
     stages = 2 + (line.bit_length() - 1) + (groups.bit_length() - 1)
     bf, f32 = jnp.bfloat16, jnp.float32
     block = (rows, width)
+    half = rows // CUT
+    pieces = (CUT, half, width)
     vm, dma = pltpu.VMEM, pltpu.SemaphoreType.DMA
     scratch = [
         vm((2 * line * rows, width), bf),
         vm((2 * rows, width), bf),
-        vm((2 * line * CUT, rows // CUT, 2 * rows), f32),
+        vm((width, 2 * rows), bf),
+        vm((line * CUT, 2 * half, 2 * rows), f32),
         vm((2 * line * rows, 2 * rows), bf),
-        vm((2 * line * CUT, 8, 2 * rows), f32),
+        vm((line * CUT, 8, 2 * rows), f32),
         vm((8, 2 * rows), f32),
         vm((8, 2 * rows), f32),
-        vm((line,) + block, bf),
-        vm((line,) + block, f32),
-        vm((line,) + block, bf),
-        vm((line,) + block, bf),
-        vm((line,) + block, bf),
-        vm((line,) + block, bf),
+        vm((line,) + pieces, bf),
+        vm((line, 2 * CUT, half, width), f32),
+        vm((line,) + pieces, bf),
+        vm((line,) + pieces, bf),
+        vm((line,) + pieces, bf),
+        vm((line,) + pieces, bf),
         vm(block, bf),
         vm(block, bf),
         vm((stages + 1, 8, 128), f32),
         vm((stages, 8, 128), f32),
-        dma((2,)), dma((2,)), dma((2 * line * CUT,)), dma((line * CUT,)), dma((line * CUT,)),
+        dma((CUT + 1,)), dma((2,)), dma((2 * line * CUT,)), dma((line * CUT,)), dma((line * CUT,)),
         dma((line * CUT,)), dma((2,)), dma((line,)), dma((line,)), dma((line * CUT,)),
         dma((line * CUT,)), dma((line * CUT,)), dma((line * CUT,)),
         dma((2,)), dma((stages,)), dma((stages,)),

time: 102 us -> 94.8 us (0.929)
  Pallas kernels: 91.6 us -> 84.2 us
    pallas_call x1, Pallas kernels: 91.6 us -> 84.2 us  [fused(): pl.pallas_call(functools.partial(kernel, line, groups), out_shape=(jax.Sh...]
where the time goes in v5:
time: 94.8 us; the launch traced here: 94.4 us
  Pallas kernels  84.2 us (89%)
  local copies, waits for them, and re-layouts  5.35 us (6%)
  between operations  4.86 us (5%)
    pallas_call x1, Pallas kernels, fused(): pl.pallas_call(functools.partial(kernel, line, groups), out_shape=(jax.Sh...  84.2 us
    unnamed x5, local copies, waits for them, and re-layouts  4.08 us

profile of v5, /device:TPU:0, one launch (start us, length us, event | category | flops | bytes accessed | tf_op | source)
XLA Modules:
  0.0 94.4 jit_solution(4332763794692219584)
XLA Ops:
  0.6 1.4 %copy.8.lists = s32[16,4]{1,0:T(8,128)} copy(s32[16,4]{0,1:T(4,128)} %param.6) | data formatting | bytes 512 | tf_op args[2]
  2.6 84.2 %shard_map.75 = (bf16[256,1024]{1,0:T(8,128)(2,1)}, bf16[256,1024]{1,0:T(8,128)(2,1)}, f32[8,128]{1,0:T(8,128)}) custom-call(bf16[256,1024]{1,0:T(8,128)(2,1)} %q_in.1, bf16[256,1024]{1,0:T(8,128)(2,1)} %p_in.1, s32[16,4]{1,0:T(8,128)} %copy.8.lists, f32[1]{0:T(128)} %bitcast.3.temp), custom_call_target="tpu_custom_call" | custom-call | tf_op jit(solution)/shard_map/pallas_call | solution.py:498
  86.9 1.3 %fusion = (f32[1,1]{1,0:T(1,128)}, f32[1,1]{1,0:T(1,128)}) fusion(f32[8,128]{1,0:T(8,128)} %get-tuple-element.9), kind=kLoop, calls=%fused_computation | loop fusion | bytes 16 | tf_op jit(solution)/shard_map/slice | solution.py:518
  89.4 0.0 copy-start
  89.4 1.9 %copy.12 = bf16[256,1024]{1,0:T(8,128)(2,1)} copy(bf16[256,1024]{1,0:T(8,128)(2,1)} %get-tuple-element.16) | data formatting | bytes 1048576
  91.4 0.0 copy-done
  91.4 0.8 copy.13
Async XLA Ops:
  89.4 1.9 %copy-start = (bf16[256,1024]{1,0:T(8,128)(2,1)S(1)}, bf16[256,1024]{1,0:T(8,128)(2,1)}, u32[]{:S(2)}) copy-start(bf16[256,1024]{1,0:T(8,128)(2,1)} %get-tuple-element.17) | copy-start | bytes 1572868

commit v6 on v5

--- a/solution.py
+++ b/solution.py
@@ -25,7 +25,7 @@
            loc_sem, q_sems, p_recv, p_right, p_left, p_core, st_sems,
            c_send, c_recv, r_send, r_recv, l_send, l_recv, g_sems, a_send, a_recv):
     rows = q_in.shape[0]
-    listed = lists.shape[1]
+    listed = lists.shape[0]
     half = rows // CUT
     wide = 2 * half
     dp = lax.axis_index("dp")
@@ -149,8 +149,8 @@
         a = jnp.int32(0)
         b = jnp.int32(0)
         for m in range(first, last):
-            a = a + jnp.where(lists[row_a, m] == block_id, 1, 0)
-            b = b + jnp.where(lists[row_b, m] == block_id, 1, 0)
+            a = a + jnp.where(lists[m, row_a] == block_id, 1, 0)
+            b = b + jnp.where(lists[m, row_b] == block_id, 1, 0)
         return jnp.where(lane < rows, a, b)
 
     def block_of(zz, kk):
@@ -267,7 +267,19 @@
         if i + 1 < len(pairs):
             a_copies[i + 1].start()
 
-    def p_grad(d):
+    def c_copy(d, c):
+        i = d * CUT + c
+        return remote(psend.at[d, c], chip_in.at[d, c], c_send.at[i], c_recv.at[i], core)
+
+    def r_copy(d, c):
+        i = d * CUT + c
+        return remote(zsend.at[d, c], zin_r.at[d, c], r_send.at[i], r_recv.at[i], right)
+
+    def l_copy(d, c):
+        i = d * CUT + c
+        return remote(zsend.at[d, c], zin_l.at[d, c], l_send.at[i], l_recv.at[i], left)
+
+    def give(d):
         pos0 = per_lane(block_of(d, 0), 0, 1) > 0
         pos1 = per_lane(block_of(d, 1), 0, 1) > 0
         for c in range(CUT):
@@ -278,30 +290,14 @@
             w1 = w[half:] - jnp.where(jnp.logical_and(ahead == c * half, pos1), 1.0, 0.0)
             wbuf[pl.ds(part * wide, half)] = w0.astype(jnp.bfloat16)
             wbuf[pl.ds(part * wide + half, half)] = w1.astype(jnp.bfloat16)
-        g = dot(wbuf[pl.ds(d * CUT * wide, CUT * wide)], qcat[...], NN) * inv_temp
-        own[d] = g.reshape(2 * CUT, half, q_in.shape[1])
-
-    def c_copy(d):
-        return remote(psend.at[d], chip_in.at[d], c_send.at[d], c_recv.at[d], core)
-
-    def r_copy(d, c):
-        i = d * CUT + c
-        return remote(zsend.at[d, c], zin_r.at[d, c], r_send.at[i], r_recv.at[i], right)
-
-    def l_copy(d, c):
-        i = d * CUT + c
-        return remote(zsend.at[d, c], zin_l.at[d, c], l_send.at[i], l_recv.at[i], left)
-
-    def give(d):
-        p_grad(d)
-        for c in range(CUT):
+            g = dot(wbuf[pl.ds(part * wide, wide)], qcat[...], NN) * inv_temp
+            own[d, pl.ds(2 * c, 2)] = g.reshape(2, half, q_in.shape[1])
             psend[d, c] = own[d, c * 2 + 1 - k].astype(jnp.bfloat16)
-        c_copy(d).start()
-
-    def take(d):
-        c_copy(d).wait_recv()
-        for c in range(CUT):
-            own[d, c * 2 + k] = own[d, c * 2 + k] + chip_in[d, c].astype(jnp.float32)
+            c_copy(d, c).start()
+
+    def take(d, c):
+        c_copy(d, c).wait_recv()
+        own[d, c * 2 + k] = own[d, c * 2 + k] + chip_in[d, c].astype(jnp.float32)
 
     for s in range(line - 1):
         dr = line - 1 - s
@@ -317,22 +313,22 @@
 
         @pl.when(dr > z)
         def _(s=s, dr=dr):
-            take(dr)
-
-            @pl.when(z == 0)
-            def _():
-                for c in range(CUT):
+            for c in range(CUT):
+                take(dr, c)
+
+                @pl.when(z == 0)
+                def _(c=c):
                     zsend[dr, c] = own[dr, c * 2 + k].astype(jnp.bfloat16)
                     if s == 0:
                         r_copy(dr, c).start()
 
         @pl.when(dl < z)
         def _(s=s, dl=dl):
-            take(dl)
-
-            @pl.when(z == line - 1)
-            def _():
-                for c in range(CUT):
+            for c in range(CUT):
+                take(dl, c)
+
+                @pl.when(z == line - 1)
+                def _(c=c):
                     zsend[dl, c] = own[dl, c * 2 + k].astype(jnp.bfloat16)
                     if s == 0:
                         l_copy(dl, c).start()
@@ -341,7 +337,8 @@
             add_up(s)
 
     give(z)
-    take(z)
+    for c in range(CUT):
+        take(z, c)
 
     def q_part(start):
         return dot(wbuf[:, pl.ds(start, rows)], pcol[...], TN) * inv_temp
@@ -442,8 +439,8 @@
 
     @pl.loop(0, line)
     def _(d):
-        c_copy(d).wait_send()
         for c in range(CUT):
+            c_copy(d, c).wait_send()
             p_copy(d, c, p_core, core).wait_send()
 
             @pl.when((d <= z) & has_r)
@@ -491,7 +488,7 @@
         vm((stages + 1, 8, 128), f32),
         vm((stages, 8, 128), f32),
         dma((CUT + 1,)), dma((2,)), dma((2 * line * CUT,)), dma((line * CUT,)), dma((line * CUT,)),
-        dma((line * CUT,)), dma((2,)), dma((line,)), dma((line,)), dma((line * CUT,)),
+        dma((line * CUT,)), dma((2,)), dma((line * CUT,)), dma((line * CUT,)), dma((line * CUT,)),
         dma((line * CUT,)), dma((line * CUT,)), dma((line * CUT,)),
         dma((2,)), dma((stages,)), dma((stages,)),
     ]
@@ -513,7 +510,7 @@
         compiler_params=pltpu.CompilerParams(
             collective_id=0, has_side_effects=True, vmem_limit_bytes=56 * 1024 * 1024
         ),
-    )(queries, passages, block_lists, inv_temp.reshape(1))
+    )(queries, passages, block_lists.T, inv_temp.reshape(1))
     pair_count = rows * groups * line * 4
     return query_grad, passage_grad, totals[0, 0] / pair_count, totals[1, 0] / pair_count
 

time: 94.8 us -> 92.4 us (0.975)
  local copies, waits for them, and re-layouts: 5.35 us -> 4 us
    unnamed x5 -> x4, local copies, waits for them, and re-layouts: 4.08 us -> 2.72 us
where the time goes in v6:
time: 92.4 us; the launch traced here: 92.2 us
  Pallas kernels  83.3 us (90%)
  between operations  4.86 us (5%)
  local copies, waits for them, and re-layouts  4 us (4%)
    pallas_call x1, Pallas kernels, fused(): pl.pallas_call(functools.partial(kernel, line, groups), out_shape=(jax.Sh...  83.3 us
    unnamed x4, local copies, waits for them, and re-layouts  2.72 us

profile of v6, /device:TPU:0, one launch (start us, length us, event | category | flops | bytes accessed | tf_op | source)
XLA Modules:
  0.0 92.2 jit_solution(17921587927069962417)
XLA Ops:
  1.3 83.3 %shard_map.75 = (bf16[256,1024]{1,0:T(8,128)(2,1)}, bf16[256,1024]{1,0:T(8,128)(2,1)}, f32[8,128]{1,0:T(8,128)}) custom-call(bf16[256,1024]{1,0:T(8,128)(2,1)} %q_in.1, bf16[256,1024]{1,0:T(8,128)(2,1)} %p_in.1, s32[4,16]{1,0:T(4,128)} %bitcast.5, f32[1]{0:T(128)} %bitcast.4.temp), custom_call_target="tpu_custom_call" | custom-call | tf_op jit(solution)/shard_map/pallas_call | solution.py:495
  84.6 1.3 %fusion = (f32[1,1]{1,0:T(1,128)}, f32[1,1]{1,0:T(1,128)}) fusion(f32[8,128]{1,0:T(8,128)} %get-tuple-element.9), kind=kLoop, calls=%fused_computation | loop fusion | bytes 16 | tf_op jit(solution)/shard_map/slice | solution.py:515
  87.2 0.0 copy-start
  87.2 1.9 %copy.11 = bf16[256,1024]{1,0:T(8,128)(2,1)} copy(bf16[256,1024]{1,0:T(8,128)(2,1)} %get-tuple-element.16) | data formatting | bytes 1048576
  89.1 0.0 copy-done
  89.1 0.8 copy.12
Async XLA Ops:
  87.2 1.9 %copy-start = (bf16[256,1024]{1,0:T(8,128)(2,1)S(1)}, bf16[256,1024]{1,0:T(8,128)(2,1)}, u32[]{:S(2)}) copy-start(bf16[256,1024]{1,0:T(8,128)(2,1)} %get-tuple-element.17) | copy-start | bytes 1572868

commit v7 on v6

--- a/solution.py
+++ b/solution.py
@@ -13,6 +13,7 @@
 TN = (((0,), (0,)), ((), ()))
 NN = (((1,), (0,)), ((), ()))
 CUT = 2
+PIECES = 4
 
 
 def dot(a, b, dims):
@@ -458,6 +459,21 @@
             @pl.when((d < z) & (has_r | (d == line - 2)))
             def _(c=c):
                 l_copy(d, c).wait_send()
+
+
+def deliver(pair_count, qg_in, pg_in, totals, qg_out, pg_out, loss, grad, sems):
+    part = qg_in.shape[0] // PIECES
+    copies = []
+    for i in range(PIECES):
+        here = pl.ds(i * part, part)
+        copies.append(pltpu.make_async_copy(qg_in.at[here], qg_out.at[here], sems.at[0, i]))
+        copies.append(pltpu.make_async_copy(pg_in.at[here], pg_out.at[here], sems.at[1, i]))
+    for copy in copies:
+        copy.start()
+    loss[0] = totals[0, 0] / pair_count
+    grad[0] = totals[1, 0] / pair_count
+    for copy in copies:
+        copy.wait()
 
 
 def fused(line, groups, queries, passages, block_lists, inv_temp):
@@ -512,7 +528,21 @@
         ),
     )(queries, passages, block_lists.T, inv_temp.reshape(1))
     pair_count = rows * groups * line * 4
-    return query_grad, passage_grad, totals[0, 0] / pair_count, totals[1, 0] / pair_count
+    hbm, smem = pl.BlockSpec(memory_space=pltpu.HBM), pl.BlockSpec(memory_space=pltpu.SMEM)
+    query_grad, passage_grad, loss_mean, temp_grad = pl.pallas_call(
+        functools.partial(deliver, pair_count),
+        out_shape=(
+            jax.ShapeDtypeStruct(block, bf),
+            jax.ShapeDtypeStruct(block, bf),
+            jax.ShapeDtypeStruct((1,), f32),
+            jax.ShapeDtypeStruct((1,), f32),
+        ),
+        in_specs=[hbm, hbm, smem],
+        out_specs=(hbm, hbm, smem, smem),
+        scratch_shapes=[dma((2, PIECES))],
+        compiler_params=pltpu.CompilerParams(vmem_limit_bytes=56 * 1024 * 1024),
+    )(query_grad, passage_grad, totals)
+    return query_grad, passage_grad, loss_mean.reshape(()), temp_grad.reshape(())
 
 
 def plain(queries, passages, block_lists, inv_temp):

time: 92.4 us -> 119 us (1.29)
  Pallas kernels: 83.3 us -> 118 us
  local copies, waits for them, and re-layouts: 4 us -> 0 us
  between operations: 4.86 us -> 1.45 us
    pallas_call x0 -> x1, Pallas kernels: none -> 34.2 us  [fused(): pl.pallas_call(functools.partial(deliver, pair_count), out_shape=(jax.Sha...]
    unnamed x4 -> x0, local copies, waits for them, and re-layouts: 2.72 us -> none
    slice x1 -> x0, local copies, waits for them, and re-layouts: 1.27 us -> none  [fused(): totals[1, 0] / pair_count]
where the time goes in v7:
time: 119 us
  Pallas kernels  118 us (99%)
  between operations  1.45 us (1%)
    pallas_call x1, Pallas kernels, fused(): pl.pallas_call(functools.partial(kernel, line, groups), out_shape=(jax.Sh...  83.3 us
    pallas_call x1, Pallas kernels, fused(): pl.pallas_call(functools.partial(deliver, pair_count), out_shape=(jax.Sha...  34.2 us

profile of v7, /device:TPU:0, one launch (start us, length us, event | category | flops | bytes accessed | tf_op | source)
XLA Modules:
  0.0 119.0 jit_solution(17270462106434624170)
XLA Ops:
  1.3 83.3 %shard_map.75 = (bf16[256,1024]{1,0:T(8,128)(2,1)}, bf16[256,1024]{1,0:T(8,128)(2,1)}, f32[8,128]{1,0:T(8,128)}) custom-call(bf16[256,1024]{1,0:T(8,128)(2,1)} %q_in.1, bf16[256,1024]{1,0:T(8,128)(2,1)} %p_in.1, s32[4,16]{1,0:T(4,128)} %bitcast.5, f32[1]{0:T(128)} %bitcast.4.temp), custom_call_target="tpu_custom_call" | custom-call | tf_op jit(solution)/shard_map/pallas_call | solution.py:511
  84.6 34.2 %shard_map.76 = (bf16[256,1024]{1,0:T(8,128)(2,1)}, bf16[256,1024]{1,0:T(8,128)(2,1)}, f32[1]{0:T(128)}, f32[1]{0:T(128)}) custom-call(bf16[256,1024]{1,0:T(8,128)(2,1)} %get-tuple-element.11.qg_in, bf16[256,1024]{1,0:T(8,128)(2,1)} %get-tuple-element.12.pg_in, f32[8,128]{1,0:T(8,128)} %get-tuple-element.13.totals), custom_call_target="tpu_custom_call" | custom-call | tf_op jit(solution)/shard_map/pallas_call | solution.py:532
